TPU v7x, 512 devices: a whole 4x8x8 slice. The times are simulated.
512 devices in a mesh: ulysses: 8 (over z_hi, core), blk: 64 (over x, z_lo, y).
Axes of the slice: x: 4, y: 8, z: 8 (z_hi: 4, z_lo: 2; z = z_hi * 2 + z_lo), core: 2. Of those that a mesh axis runs over, the one named last changes fastest.
Arguments:
- queries: bfloat16 [65536, 1024], P(('blk', 'ulysses')), may hold values from -6 to 6
- key_rows: bfloat16 [65536, 1024], P(('blk', 'ulysses')), may hold values from -6 to 6
- value_rows: bfloat16 [65536, 1024], P(('blk', 'ulysses')), may hold values from -6 to 6
- attn_output: bfloat16 [65536, 1024], P(('blk', 'ulysses')), may hold values from -2 to 2
- grad_output: bfloat16 [65536, 1024], P(('blk', 'ulysses')), may hold values from -48 to 48
- logsumexp: float32 [65536, 8], P('blk', 'ulysses')
- positions: int32 [65536], replicated, may hold values from 0 to 4095, as said below
Outputs:
- grad_queries: bfloat16 [65536, 1024], P(('blk', 'ulysses'))
- grad_keys: bfloat16 [65536, 1024], P(('blk', 'ulysses'))
- grad_values: bfloat16 [65536, 1024], P(('blk', 'ulysses'))
Inputs may be any that keep to these rules, and one draw needn't show every extreme that they name: For each s below 16, the runs s, s + 16, ..., s + 48 of 1024 rows hold one sequence of 4096 positions, each position once. Each such run holds, in order, the a-th and then the (7 - a)-th block of 512 consecutive positions, each ascending, with a different a for each run of the sequence.
All inputs are finite; a program needn't handle non-finite values.
Results may differ from a plain program's by a relative error of at most 0.0057.
Values may be sent and summed in bfloat16 or wider, within the bound.
No kernel may reach another device: no remote copies, remote signals or barrier semaphores. Data moves between devices by JAX's collectives and lax.ppermute only.
A program may use at most 64 MiB of HBM per device.

v0:
```python
import jax
import jax.numpy as jnp
from jax import lax
from jax.sharding import PartitionSpec as P

SPAN = 4


def passed_along(value, axis, steps):
    count = lax.axis_size(axis)
    pairs = [(source, (source + steps) % count) for source in range(count)]
    return lax.ppermute(value, axis, pairs)


def block_length(row_total):
    length = row_total
    while length > 512 and length % 2 == 0:
        length = length // 2
    return length


def tile_grads(
    query_tile, cotangent_tile, lse_tile, delta_tile, query_place, key_tile, value_tile, key_place
):
    scaling = query_tile.shape[-1] ** (-0.5)
    scores = (
        jnp.einsum("qhd,khd->hqk", query_tile, key_tile, preferred_element_type=jnp.float32)
        * scaling
    )
    visible = query_place[:, None] >= key_place[None, :]
    probs = jnp.where(visible[None], jnp.exp(scores - lse_tile.T[:, :, None]), jnp.float32(0.0))
    probs_low = probs.astype(jnp.bfloat16)
    grad_probs = jnp.einsum(
        "qhd,khd->hqk", cotangent_tile, value_tile, preferred_element_type=jnp.float32
    )
    grad_scores = (probs * (grad_probs - delta_tile.T[:, :, None])).astype(jnp.bfloat16)
    grad_query = (
        jnp.einsum("hqk,khd->qhd", grad_scores, key_tile, preferred_element_type=jnp.float32)
        * scaling
    )
    grad_key = (
        jnp.einsum("hqk,qhd->khd", grad_scores, query_tile, preferred_element_type=jnp.float32)
        * scaling
    )
    grad_value = jnp.einsum(
        "hqk,qhd->khd", probs_low, cotangent_tile, preferred_element_type=jnp.float32
    )
    return (grad_query, grad_key, grad_value)


def visit(
    query_tile, cotangent_tile, lse_tile, delta_tile, query_place, key_tile, value_tile, key_place
):
    key_count, heads_dev, head_dim = key_tile.shape
    length = block_length(key_count)
    block_total = key_count // length

    def key_step(running, tiles):
        key_part, value_part, place_part = tiles
        grads = tile_grads(
            query_tile,
            cotangent_tile,
            lse_tile,
            delta_tile,
            query_place,
            key_part,
            value_part,
            place_part,
        )
        return (running + grads[0], (grads[1], grads[2]))

    start_query = jnp.zeros(query_tile.shape, jnp.float32)
    grad_query, (grad_key, grad_value) = lax.scan(
        key_step,
        start_query,
        (
            key_tile.reshape(block_total, length, heads_dev, head_dim),
            value_tile.reshape(block_total, length, heads_dev, head_dim),
            key_place.reshape(block_total, length),
        ),
    )
    return (
        grad_query,
        grad_key.reshape(key_count, heads_dev, head_dim),
        grad_value.reshape(key_count, heads_dev, head_dim),
    )


def per_device(queries, key_rows, value_rows, attn_output, grad_output, logsumexp, positions):
    heads_dev = logsumexp.shape[1]
    moved = (
        lax.all_to_all(queries, "ulysses", split_axis=1, concat_axis=0, tiled=True),
        lax.all_to_all(key_rows, "ulysses", split_axis=1, concat_axis=0, tiled=True),
        lax.all_to_all(value_rows, "ulysses", split_axis=1, concat_axis=0, tiled=True),
        lax.all_to_all(attn_output, "ulysses", split_axis=1, concat_axis=0, tiled=True),
        lax.all_to_all(grad_output, "ulysses", split_axis=1, concat_axis=0, tiled=True),
    )
    row_count = moved[0].shape[0]
    head_dim = moved[0].shape[1] // heads_dev
    query_heads = moved[0].reshape(row_count, heads_dev, head_dim)
    key_heads = moved[1].reshape(row_count, heads_dev, head_dim)
    value_heads = moved[2].reshape(row_count, heads_dev, head_dim)
    output_heads = moved[3].reshape(row_count, heads_dev, head_dim)
    cotangent_heads = moved[4].reshape(row_count, heads_dev, head_dim)
    delta_own = jnp.sum(
        cotangent_heads.astype(jnp.float32) * output_heads.astype(jnp.float32), axis=-1
    )
    blk_count = lax.axis_size("blk")
    stride = blk_count // SPAN
    blk_place = lax.axis_index("blk")

    def rows_of(holder):
        return lax.dynamic_slice_in_dim(positions, holder * row_count, row_count)

    own_place = rows_of(blk_place)
    zeros_grad = jnp.zeros((row_count, heads_dev, head_dim), jnp.float32)
    visiting = (query_heads, cotangent_heads)
    carried = (zeros_grad, logsumexp, delta_own)
    grad_key = zeros_grad
    grad_value = zeros_grad
    for turn in range(SPAN):
        holder = (blk_place - turn * stride) % blk_count
        grads = visit(
            visiting[0],
            visiting[1],
            carried[1],
            carried[2],
            rows_of(holder),
            key_heads,
            value_heads,
            own_place,
        )
        grad_key = grad_key + grads[1]
        grad_value = grad_value + grads[2]
        if turn + 1 < SPAN:
            visiting = passed_along((visiting[0], visiting[1]), "blk", stride)
        carried = passed_along((carried[0] + grads[0], carried[1], carried[2]), "blk", stride)
    grad_query = carried[0]
    width = heads_dev * head_dim
    low_query = grad_query.astype(jnp.bfloat16).reshape(row_count, width)
    low_key = grad_key.astype(jnp.bfloat16).reshape(row_count, width)
    low_value = grad_value.astype(jnp.bfloat16).reshape(row_count, width)
    back = (
        lax.all_to_all(low_query, "ulysses", split_axis=0, concat_axis=1, tiled=True),
        lax.all_to_all(low_key, "ulysses", split_axis=0, concat_axis=1, tiled=True),
        lax.all_to_all(low_value, "ulysses", split_axis=0, concat_axis=1, tiled=True),
    )
    return (back[0], back[1], back[2])


def solution(mesh):
    placed = (
        P(("blk", "ulysses"), None),
        P(("blk", "ulysses"), None),
        P(("blk", "ulysses"), None),
        P(("blk", "ulysses"), None),
        P(("blk", "ulysses"), None),
        P("blk", "ulysses"),
        P(),
    )
    return jax.shard_map(
        per_device,
        mesh=mesh,
        in_specs=placed,
        out_specs=(
            P(("blk", "ulysses"), None),
            P(("blk", "ulysses"), None),
            P(("blk", "ulysses"), None),
        ),
        check_vma=False,
    )
```

profile of v0, /device:TPU:56, one launch (start us, length us, event | category | flops | bytes accessed | tf_op | source)
XLA Modules:
  0.0 265.4 jit_solution(11372489214581865836)
XLA Ops:
  2.5 10.3 %all-to-all-start = ((bf16[128,8,128]{0,2,1:T(8,128)(2,1)}), bf16[128,8,128]{0,2,1:T(8,128)(2,1)S(1)}, u32[]{:S(2)}, u32[]{:S(2)}) async-start(bf16[128,8,128]{0,2,1:T(8,128)(2,1)} %bitcast), calls=%async_computation | async-start | bytes 524288 | tf_op jit(solution)/shard_map/all_to_all | solution.py:93
  14.6 10.9 %all-to-all-done = bf16[128,8,128]{0,2,1:T(8,128)(2,1)S(1)} async-done(((bf16[128,8,128]{0,2,1:T(8,128)(2,1)}), bf16[128,8,128]{0,2,1:T(8,128)(2,1)S(1)}, u32[]{:S(2)}, u32[]{:S(2)}) %all-to-all-start) | async-done | bytes 262176 | tf_op jit(solution)/shard_map/all_to_all | solution.py:93
  25.6 3.4 %all-to-all-start.1 = ((bf16[128,8,128]{0,2,1:T(8,128)(2,1)}), bf16[128,8,128]{0,2,1:T(8,128)(2,1)S(1)}, u32[]{:S(2)}, u32[]{:S(2)}) async-start(bf16[128,8,128]{0,2,1:T(8,128)(2,1)} %bitcast.4), calls=%async_computation.1 | async-start | bytes 524288 | tf_op jit(solution)/shard_map/all_to_all | solution.py:92
  29.9 11.2 %all-to-all-done.1 = bf16[128,8,128]{0,2,1:T(8,128)(2,1)S(1)} async-done(((bf16[128,8,128]{0,2,1:T(8,128)(2,1)}), bf16[128,8,128]{0,2,1:T(8,128)(2,1)S(1)}, u32[]{:S(2)}, u32[]{:S(2)}) %all-to-all-start.1) | async-done | bytes 262176 | tf_op jit(solution)/shard_map/all_to_all | solution.py:92
  41.0 3.4 %all-to-all-start.3 = ((bf16[128,8,128]{0,2,1:T(8,128)(2,1)}), bf16[128,8,128]{0,2,1:T(8,128)(2,1)S(1)}, u32[]{:S(2)}, u32[]{:S(2)}) async-start(bf16[128,8,128]{0,2,1:T(8,128)(2,1)} %bitcast.11), calls=%async_computation.3 | async-start | bytes 524288 | tf_op jit(solution)/shard_map/all_to_all | solution.py:96
  45.3 11.7 %all-to-all-done.3 = bf16[128,8,128]{0,2,1:T(8,128)(2,1)S(1)} async-done(((bf16[128,8,128]{0,2,1:T(8,128)(2,1)}), bf16[128,8,128]{0,2,1:T(8,128)(2,1)S(1)}, u32[]{:S(2)}, u32[]{:S(2)}) %all-to-all-start.3) | async-done | bytes 262176 | tf_op jit(solution)/shard_map/all_to_all | solution.py:96
  57.0 3.4 %all-to-all-start.4 = ((bf16[128,8,128]{0,2,1:T(8,128)(2,1)}), bf16[128,8,128]{0,2,1:T(8,128)(2,1)S(1)}, u32[]{:S(2)}, u32[]{:S(2)}) async-start(bf16[128,8,128]{0,2,1:T(8,128)(2,1)} %bitcast.14), calls=%async_computation.4 | async-start | bytes 524288 | tf_op jit(solution)/shard_map/all_to_all | solution.py:95
  61.3 11.3 %all-to-all-done.4 = bf16[128,8,128]{0,2,1:T(8,128)(2,1)S(1)} async-done(((bf16[128,8,128]{0,2,1:T(8,128)(2,1)}), bf16[128,8,128]{0,2,1:T(8,128)(2,1)S(1)}, u32[]{:S(2)}, u32[]{:S(2)}) %all-to-all-start.4) | async-done | bytes 262176 | tf_op jit(solution)/shard_map/all_to_all | solution.py:95
  72.6 3.4 %all-to-all-start.2 = ((bf16[128,8,128]{0,2,1:T(8,128)(2,1)}), bf16[128,8,128]{0,2,1:T(8,128)(2,1)S(1)}, u32[]{:S(2)}, u32[]{:S(2)}) async-start(bf16[128,8,128]{0,2,1:T(8,128)(2,1)} %bitcast.7), calls=%async_computation.2 | async-start | bytes 524288 | tf_op jit(solution)/shard_map/all_to_all | solution.py:94
  76.0 3.4 %collective-permute-start.2 = (f32[1024,1]{0,1:T(1,128)S(1)}, f32[1024,1]{0,1:T(1,128)S(1)}, u32[]{:S(2)}, u32[]{:S(2)}) collective-permute-start(f32[1024,1]{0,1:T(1,128)S(1)} %copy-done.29), channel_id=1, source_target_pairs={{0,16},{1,17},{2,18},{3,19},{4,20},{5,21},{6,22},{7,23},{8,24},{9,... | collective-permute-start | bytes 12296 | tf_op jit(solution)/shard_map/ppermute | solution.py:12
  79.5 3.2 %collective-permute-done.2 = f32[1024,1]{0,1:T(1,128)S(1)} collective-permute-done((f32[1024,1]{0,1:T(1,128)S(1)}, f32[1024,1]{0,1:T(1,128)S(1)}, u32[]{:S(2)}, u32[]{:S(2)}) %collective-permute-start.2) | collective-permute-done | bytes 4128 | tf_op jit(solution)/shard_map/ppermute | solution.py:12
  85.0 3.4 %collective-permute-start.4 = (f32[1024,1]{0,1:T(1,128)S(1)}, f32[1024,1]{0,1:T(1,128)S(1)}, u32[]{:S(2)}, u32[]{:S(2)}) collective-permute-start(f32[1024,1]{0,1:T(1,128)S(1)} %bitcast.406), channel_id=1, source_target_pairs={{0,16},{1,17},{2,18},{3,19},{4,20},{5,21},{6,22},{7,23},{8,24},{9,... | collective-permute-start | bytes 12296 | tf_op jit(solution)/shard_map/ppermute | solution.py:12
  89.6 2.8 %collective-permute-start.12 = (f32[1024,1]{0,1:T(1,128)}, f32[1024,1]{0,1:T(1,128)S(1)}, u32[]{:S(2)}, u32[]{:S(2)}) collective-permute-start(f32[1024,1]{0,1:T(1,128)} %collective-permute-done.7), channel_id=1, source_target_pairs={{0,16},{1,17},{2,18},{3,19},{4,20},{5,21},{6,22},{7,23},{8,24},{9,... | collective-permute-start | bytes 12296 | tf_op jit(solution)/shard_map/ppermute | solution.py:12
  95.1 3.6 %collective-permute-start.1 = (bf16[1024,1,128]{2,0,1:T(8,128)(2,1)}, bf16[1024,1,128]{2,0,1:T(8,128)(2,1)}, u32[]{:S(2)}, u32[]{:S(2)}) collective-permute-start(bf16[1024,1,128]{2,0,1:T(8,128)(2,1)} %bitcast.6), channel_id=1, source_target_pairs={{0,16},{1,17},{2,18},{3,19},{4,20},{5,21},{6,22},{7,23},{8,24},{9,... | collective-permute-start | bytes 786440 | tf_op jit(solution)/shard_map/ppermute | solution.py:12
  100.9 3.7 %collective-permute-start.9 = (f32[1024,1]{0,1:T(1,128)S(1)}, f32[1024,1]{0,1:T(1,128)}, u32[]{:S(2)}, u32[]{:S(2)}) collective-permute-start(f32[1024,1]{0,1:T(1,128)S(1)} %collective-permute-done.4), channel_id=1, source_target_pairs={{0,16},{1,17},{2,18},{3,19},{4,20},{5,21},{6,22},{7,23},{8,24},{9,... | collective-permute-start | bytes 12296 | tf_op jit(solution)/shard_map/ppermute | solution.py:12
  106.3 17.1 %while.60 = (s32[]{:T(128)}, f32[1024,1,128]{0,2,1:T(8,128)}, f32[2,512,1,128]{3,1,2,0:T(8,128)}, f32[2,512,1,128]{3,1,2,0:T(8,128)}, bf16[2,512,1,128]{3,1,2,0:...) while((s32[]{:T(128)}, f32[1024,1,128]{0,2,1:T(8,128)}, ...), condition=%wide.region_2.3_spmd.clone, body=%wide.region_1.2_spmd.clone.sunk | while | flops 675741696 | bytes 21907772 | solution.py:73
  123.4 2.8 %collective-permute-start = (f32[1024,1,128]{0,2,1:T(8,128)}, f32[1024,1,128]{0,2,1:T(8,128)}, u32[]{:S(2)}, u32[]{:S(2)}) collective-permute-start(f32[1024,1,128]{0,2,1:T(8,128)} %get-tuple-element.259), channel_id=1, source_target_pairs={{0,16},{1,17},{2,18},{3,19},{4,20},{5,21},{6,22},{7,23},{8,24},{9,... | collective-permute-start | bytes 1572872 | tf_op jit(solution)/shard_map/ppermute | solution.py:12
  126.2 3.6 %collective-permute-start.14 = (f32[1024,1]{0,1:T(1,128)}, f32[1024,1]{0,1:T(1,128)S(1)}, u32[]{:S(2)}, u32[]{:S(2)}) collective-permute-start(f32[1024,1]{0,1:T(1,128)} %collective-permute-done.9), channel_id=1, source_target_pairs={{0,16},{1,17},{2,18},{3,19},{4,20},{5,21},{6,22},{7,23},{8,24},{9,... | collective-permute-start | bytes 12296 | tf_op jit(solution)/shard_map/ppermute | solution.py:12
  132.0 3.7 %collective-permute-start.8 = (bf16[1024,1,128]{2,0,1:T(8,128)(2,1)}, bf16[1024,1,128]{2,0,1:T(8,128)(2,1)}, u32[]{:S(2)}, u32[]{:S(2)}) collective-permute-start(bf16[1024,1,128]{2,0,1:T(8,128)(2,1)} %collective-permute-done.3), channel_id=1, source_target_pairs={{0,16},{1,17},{2,18},{3,19},{4,20},{5,21},{6,22},{7,23},{8,24},{9,... | collective-permute-start | bytes 786440 | tf_op jit(solution)/shard_map/ppermute | solution.py:12
  137.4 17.1 %while.61 = (s32[]{:T(128)}, f32[1024,1,128]{0,2,1:T(8,128)}, f32[2,512,1,128]{3,1,2,0:T(8,128)}, f32[2,512,1,128]{3,1,2,0:T(8,128)}, bf16[2,512,1,128]{3,1,2,0:...) while((s32[]{:T(128)}, f32[1024,1,128]{0,2,1:T(8,128)}, ...), condition=%wide.region_4.5_spmd.clone, body=%wide.region_3.4_spmd.clone.sunk | while | flops 675741696 | bytes 21907772 | solution.py:73
  156.6 2.8 %collective-permute-start.5 = (f32[1024,1,128]{0,2,1:T(8,128)}, f32[1024,1,128]{0,2,1:T(8,128)}, u32[]{:S(2)}, u32[]{:S(2)}) collective-permute-start(f32[1024,1,128]{0,2,1:T(8,128)} %add.117), channel_id=1, source_target_pairs={{0,16},{1,17},{2,18},{3,19},{4,20},{5,21},{6,22},{7,23},{8,24},{9,... | collective-permute-start | bytes 1572872 | tf_op jit(solution)/shard_map/ppermute | solution.py:12
  159.4 3.6 %collective-permute-start.11 = (bf16[1024,1,128]{2,0,1:T(8,128)(2,1)}, bf16[1024,1,128]{2,0,1:T(8,128)(2,1)}, u32[]{:S(2)}, u32[]{:S(2)}) collective-permute-start(bf16[1024,1,128]{2,0,1:T(8,128)(2,1)} %collective-permute-done.6), channel_id=1, source_target_pairs={{0,16},{1,17},{2,18},{3,19},{4,20},{5,21},{6,22},{7,23},{8,24},{9,... | collective-permute-start | bytes 786440 | tf_op jit(solution)/shard_map/ppermute | solution.py:12
  166.8 17.1 %while.62 = (s32[]{:T(128)}, f32[1024,1,128]{0,2,1:T(8,128)}, f32[2,512,1,128]{3,1,2,0:T(8,128)}, f32[2,512,1,128]{3,1,2,0:T(8,128)}, bf16[2,512,1,128]{3,1,2,0:...) while((s32[]{:T(128)}, f32[1024,1,128]{0,2,1:T(8,128)}, ...), condition=%wide.region_6.7_spmd.clone, body=%wide.region_5.6_spmd.clone.sunk | while | flops 675741696 | bytes 21907772 | solution.py:73
  185.7 17.2 %while.63 = (s32[]{:T(128)}, f32[1024,1,128]{0,2,1:T(8,128)}, f32[2,512,1,128]{3,1,2,0:T(8,128)}, f32[2,512,1,128]{3,1,2,0:T(8,128)}, bf16[2,512,1,128]{3,1,2,0:...) while((s32[]{:T(128)}, f32[1024,1,128]{0,2,1:T(8,128)}, ...), condition=%wide.region_8.9_spmd.clone, body=%wide.region_7.8_spmd.clone.sunk | while | flops 675741696 | bytes 21907772 | solution.py:73
  205.3 7.1 %all-to-all-start.6 = ((bf16[8,128,128]{2,1,0:T(8,128)(2,1)}), bf16[8,128,128]{2,1,0:T(8,128)(2,1)S(1)}, u32[]{:S(2)}, u32[]{:S(2)}) async-start(bf16[8,128,128]{2,1,0:T(8,128)(2,1)} %bitcast.26), calls=%async_computation.6 | async-start | bytes 524288 | tf_op jit(solution)/shard_map/all_to_all | solution.py:145
  214.4 3.7 %collective-permute-start.10 = (f32[1024,1,128]{0,2,1:T(8,128)}, f32[1024,1,128]{0,2,1:T(8,128)}, u32[]{:S(2)}, u32[]{:S(2)}) collective-permute-start(f32[1024,1,128]{0,2,1:T(8,128)} %add.120), channel_id=1, source_target_pairs={{0,16},{1,17},{2,18},{3,19},{4,20},{5,21},{6,22},{7,23},{8,24},{9,... | collective-permute-start | bytes 1572872 | tf_op jit(solution)/shard_map/ppermute | solution.py:12
  218.9 6.1 %all-to-all-done.6 = bf16[8,128,128]{2,1,0:T(8,128)(2,1)S(1)} async-done(((bf16[8,128,128]{2,1,0:T(8,128)(2,1)}), bf16[8,128,128]{2,1,0:T(8,128)(2,1)S(1)}, u32[]{:S(2)}, u32[]{:S(2)}) %all-to-all-start.6) | async-done | bytes 262176 | tf_op jit(solution)/shard_map/all_to_all | solution.py:145
  225.1 3.4 %all-to-all-start.7 = ((bf16[8,128,128]{2,1,0:T(8,128)(2,1)}), bf16[8,128,128]{2,1,0:T(8,128)(2,1)S(1)}, u32[]{:S(2)}, u32[]{:S(2)}) async-start(bf16[8,128,128]{2,1,0:T(8,128)(2,1)} %bitcast.29), calls=%async_computation.7 | async-start | bytes 524288 | tf_op jit(solution)/shard_map/all_to_all | solution.py:146
  228.5 3.7 %collective-permute-done.10 = f32[1024,1,128]{0,2,1:T(8,128)} collective-permute-done((f32[1024,1,128]{0,2,1:T(8,128)}, f32[1024,1,128]{0,2,1:T(8,128)}, u32[]{:S(2)}, u32[]{:S(2)}) %collective-permute-start.10) | collective-permute-done | bytes 524320 | tf_op jit(solution)/shard_map/ppermute | solution.py:12
  235.7 8.6 %collective-permute-done.15 = bf16[1024,1,128]{0,2,1:T(8,128)(2,1)S(1)} collective-permute-done((bf16[1024,1,128]{0,2,1:T(8,128)(2,1)S(1)}, bf16[1024,1,128]{0,2,1:T(8,128)(2,1)S(1)}, u32[]{:S(2)}, u32[]{:S(2)}) %collective-permute-start.15) | collective-permute-done | bytes 262176 | tf_op jit(solution)/shard_map/ppermute | solution.py:12
  245.2 6.5 %all-to-all-start.5 = ((bf16[8,128,128]{2,1,0:T(8,128)(2,1)}), bf16[8,128,128]{2,1,0:T(8,128)(2,1)S(1)}, u32[]{:S(2)}, u32[]{:S(2)}) async-start(bf16[8,128,128]{2,1,0:T(8,128)(2,1)} %bitcast.23), calls=%async_computation.5 | async-start | bytes 524288 | tf_op jit(solution)/shard_map/all_to_all | solution.py:144
  253.7 10.6 %all-to-all-done.5 = bf16[8,128,128]{2,1,0:T(8,128)(2,1)S(1)} async-done(((bf16[8,128,128]{2,1,0:T(8,128)(2,1)}), bf16[8,128,128]{2,1,0:T(8,128)(2,1)S(1)}, u32[]{:S(2)}, u32[]{:S(2)}) %all-to-all-start.5) | async-done | bytes 262176 | tf_op jit(solution)/shard_map/all_to_all | solution.py:144
  (204 shorter events, 108.1 us)
Async XLA Ops:
  0.6 28.4 %copy-start.26 = (bf16[128,1024]{1,0:T(8,128)(2,1)S(1)}, bf16[128,1024]{1,0:T(8,128)(2,1)}, u32[]{:S(2)}) copy-start(bf16[128,1024]{1,0:T(8,128)(2,1)} %param.19) | copy-start | bytes 786436
  0.6 43.8 %copy-start.27 = (bf16[128,1024]{1,0:T(8,128)(2,1)S(1)}, bf16[128,1024]{1,0:T(8,128)(2,1)}, u32[]{:S(2)}) copy-start(bf16[128,1024]{1,0:T(8,128)(2,1)} %param.18) | copy-start | bytes 786436
  0.7 59.8 %copy-start.28 = (bf16[128,1024]{1,0:T(8,128)(2,1)S(1)}, bf16[128,1024]{1,0:T(8,128)(2,1)}, u32[]{:S(2)}) copy-start(bf16[128,1024]{1,0:T(8,128)(2,1)} %param.17) | copy-start | bytes 786436
  2.5 23.1 %all-to-all-start = ((bf16[128,8,128]{0,2,1:T(8,128)(2,1)}), bf16[128,8,128]{0,2,1:T(8,128)(2,1)S(1)}, u32[]{:S(2)}, u32[]{:S(2)}) async-start(bf16[128,8,128]{0,2,1:T(8,128)(2,1)} %bitcast), calls=%async_computation | async-start | bytes 524288 | tf_op jit(solution)/shard_map/all_to_all | solution.py:93
  12.8 63.2 %copy-start.29 = (f32[1024,1]{0,1:T(1,128)S(1)}, f32[1024,1]{0,1:T(1,128)}, u32[]{:S(2)}) copy-start(f32[1024,1]{0,1:T(1,128)} %param.20) | copy-start | bytes 12292
  25.6 15.4 %all-to-all-start.1 = ((bf16[128,8,128]{0,2,1:T(8,128)(2,1)}), bf16[128,8,128]{0,2,1:T(8,128)(2,1)S(1)}, u32[]{:S(2)}, u32[]{:S(2)}) async-start(bf16[128,8,128]{0,2,1:T(8,128)(2,1)} %bitcast.4), calls=%async_computation.1 | async-start | bytes 524288 | tf_op jit(solution)/shard_map/all_to_all | solution.py:92
  41.0 16.0 %all-to-all-start.3 = ((bf16[128,8,128]{0,2,1:T(8,128)(2,1)}), bf16[128,8,128]{0,2,1:T(8,128)(2,1)S(1)}, u32[]{:S(2)}, u32[]{:S(2)}) async-start(bf16[128,8,128]{0,2,1:T(8,128)(2,1)} %bitcast.11), calls=%async_computation.3 | async-start | bytes 524288 | tf_op jit(solution)/shard_map/all_to_all | solution.py:96
  57.0 15.6 %all-to-all-start.4 = ((bf16[128,8,128]{0,2,1:T(8,128)(2,1)}), bf16[128,8,128]{0,2,1:T(8,128)(2,1)S(1)}, u32[]{:S(2)}, u32[]{:S(2)}) async-start(bf16[128,8,128]{0,2,1:T(8,128)(2,1)} %bitcast.14), calls=%async_computation.4 | async-start | bytes 524288 | tf_op jit(solution)/shard_map/all_to_all | solution.py:95
  72.6 20.8 %all-to-all-start.2 = ((bf16[128,8,128]{0,2,1:T(8,128)(2,1)}), bf16[128,8,128]{0,2,1:T(8,128)(2,1)S(1)}, u32[]{:S(2)}, u32[]{:S(2)}) async-start(bf16[128,8,128]{0,2,1:T(8,128)(2,1)} %bitcast.7), calls=%async_computation.2 | async-start | bytes 524288 | tf_op jit(solution)/shard_map/all_to_all | solution.py:94
  76.0 6.7 %collective-permute-start.2 = (f32[1024,1]{0,1:T(1,128)S(1)}, f32[1024,1]{0,1:T(1,128)S(1)}, u32[]{:S(2)}, u32[]{:S(2)}) collective-permute-start(f32[1024,1]{0,1:T(1,128)S(1)} %copy-done.29), channel_id=1, source_target_pairs={{0,16},{1,17},{2,18},{3,19},{4,20},{5,21},{6,22},{7,23},{8,24},{9,... | collective-permute-start | bytes 12296 | tf_op jit(solution)/shard_map/ppermute | solution.py:12
  82.8 6.8 %collective-permute-start.7 = (f32[1024,1]{0,1:T(1,128)S(1)}, f32[1024,1]{0,1:T(1,128)}, u32[]{:S(2)}, u32[]{:S(2)}) collective-permute-start(f32[1024,1]{0,1:T(1,128)S(1)} %collective-permute-done.2), channel_id=1, source_target_pairs={{0,16},{1,17},{2,18},{3,19},{4,20},{5,21},{6,22},{7,23},{8,24},{9,... | collective-permute-start | bytes 12296 | tf_op jit(solution)/shard_map/ppermute | solution.py:12
  85.0 15.9 %collective-permute-start.4 = (f32[1024,1]{0,1:T(1,128)S(1)}, f32[1024,1]{0,1:T(1,128)S(1)}, u32[]{:S(2)}, u32[]{:S(2)}) collective-permute-start(f32[1024,1]{0,1:T(1,128)S(1)} %bitcast.406), channel_id=1, source_target_pairs={{0,16},{1,17},{2,18},{3,19},{4,20},{5,21},{6,22},{7,23},{8,24},{9,... | collective-permute-start | bytes 12296 | tf_op jit(solution)/shard_map/ppermute | solution.py:12
  89.6 94.4 %collective-permute-start.12 = (f32[1024,1]{0,1:T(1,128)}, f32[1024,1]{0,1:T(1,128)S(1)}, u32[]{:S(2)}, u32[]{:S(2)}) collective-permute-start(f32[1024,1]{0,1:T(1,128)} %collective-permute-done.7), channel_id=1, source_target_pairs={{0,16},{1,17},{2,18},{3,19},{4,20},{5,21},{6,22},{7,23},{8,24},{9,... | collective-permute-start | bytes 12296 | tf_op jit(solution)/shard_map/ppermute | solution.py:12
  95.1 34.7 %collective-permute-start.1 = (bf16[1024,1,128]{2,0,1:T(8,128)(2,1)}, bf16[1024,1,128]{2,0,1:T(8,128)(2,1)}, u32[]{:S(2)}, u32[]{:S(2)}) collective-permute-start(bf16[1024,1,128]{2,0,1:T(8,128)(2,1)} %bitcast.6), channel_id=1, source_target_pairs={{0,16},{1,17},{2,18},{3,19},{4,20},{5,21},{6,22},{7,23},{8,24},{9,... | collective-permute-start | bytes 786440 | tf_op jit(solution)/shard_map/ppermute | solution.py:12
  98.7 33.3 %collective-permute-start.3 = (bf16[1024,1,128]{2,0,1:T(8,128)(2,1)}, bf16[1024,1,128]{2,0,1:T(8,128)(2,1)}, u32[]{:S(2)}, u32[]{:S(2)}) collective-permute-start(bf16[1024,1,128]{2,0,1:T(8,128)(2,1)} %bitcast.13), channel_id=1, source_target_pairs={{0,16},{1,17},{2,18},{3,19},{4,20},{5,21},{6,22},{7,23},{8,24},{9,... | collective-permute-start | bytes 786440 | tf_op jit(solution)/shard_map/ppermute | solution.py:12
  100.9 25.3 %collective-permute-start.9 = (f32[1024,1]{0,1:T(1,128)S(1)}, f32[1024,1]{0,1:T(1,128)}, u32[]{:S(2)}, u32[]{:S(2)}) collective-permute-start(f32[1024,1]{0,1:T(1,128)S(1)} %collective-permute-done.4), channel_id=1, source_target_pairs={{0,16},{1,17},{2,18},{3,19},{4,20},{5,21},{6,22},{7,23},{8,24},{9,... | collective-permute-start | bytes 12296 | tf_op jit(solution)/shard_map/ppermute | solution.py:12
  123.4 31.2 %collective-permute-start = (f32[1024,1,128]{0,2,1:T(8,128)}, f32[1024,1,128]{0,2,1:T(8,128)}, u32[]{:S(2)}, u32[]{:S(2)}) collective-permute-start(f32[1024,1,128]{0,2,1:T(8,128)} %get-tuple-element.259), channel_id=1, source_target_pairs={{0,16},{1,17},{2,18},{3,19},{4,20},{5,21},{6,22},{7,23},{8,24},{9,... | collective-permute-start | bytes 1572872 | tf_op jit(solution)/shard_map/ppermute | solution.py:12
  126.2 57.8 %collective-permute-start.14 = (f32[1024,1]{0,1:T(1,128)}, f32[1024,1]{0,1:T(1,128)S(1)}, u32[]{:S(2)}, u32[]{:S(2)}) collective-permute-start(f32[1024,1]{0,1:T(1,128)} %collective-permute-done.9), channel_id=1, source_target_pairs={{0,16},{1,17},{2,18},{3,19},{4,20},{5,21},{6,22},{7,23},{8,24},{9,... | collective-permute-start | bytes 12296 | tf_op jit(solution)/shard_map/ppermute | solution.py:12
  129.8 29.6 %collective-permute-start.6 = (bf16[1024,1,128]{2,0,1:T(8,128)(2,1)}, bf16[1024,1,128]{2,0,1:T(8,128)(2,1)}, u32[]{:S(2)}, u32[]{:S(2)}) collective-permute-start(bf16[1024,1,128]{2,0,1:T(8,128)(2,1)} %collective-permute-done.1), channel_id=1, source_target_pairs={{0,16},{1,17},{2,18},{3,19},{4,20},{5,21},{6,22},{7,23},{8,24},{9,... | collective-permute-start | bytes 786440 | tf_op jit(solution)/shard_map/ppermute | solution.py:12
  132.0 31.0 %collective-permute-start.8 = (bf16[1024,1,128]{2,0,1:T(8,128)(2,1)}, bf16[1024,1,128]{2,0,1:T(8,128)(2,1)}, u32[]{:S(2)}, u32[]{:S(2)}) collective-permute-start(bf16[1024,1,128]{2,0,1:T(8,128)(2,1)} %collective-permute-done.3), channel_id=1, source_target_pairs={{0,16},{1,17},{2,18},{3,19},{4,20},{5,21},{6,22},{7,23},{8,24},{9,... | collective-permute-start | bytes 786440 | tf_op jit(solution)/shard_map/ppermute | solution.py:12
  156.6 55.8 %collective-permute-start.5 = (f32[1024,1,128]{0,2,1:T(8,128)}, f32[1024,1,128]{0,2,1:T(8,128)}, u32[]{:S(2)}, u32[]{:S(2)}) collective-permute-start(f32[1024,1,128]{0,2,1:T(8,128)} %add.117), channel_id=1, source_target_pairs={{0,16},{1,17},{2,18},{3,19},{4,20},{5,21},{6,22},{7,23},{8,24},{9,... | collective-permute-start | bytes 1572872 | tf_op jit(solution)/shard_map/ppermute | solution.py:12
  159.4 24.6 %collective-permute-start.11 = (bf16[1024,1,128]{2,0,1:T(8,128)(2,1)}, bf16[1024,1,128]{2,0,1:T(8,128)(2,1)}, u32[]{:S(2)}, u32[]{:S(2)}) collective-permute-start(bf16[1024,1,128]{2,0,1:T(8,128)(2,1)} %collective-permute-done.6), channel_id=1, source_target_pairs={{0,16},{1,17},{2,18},{3,19},{4,20},{5,21},{6,22},{7,23},{8,24},{9,... | collective-permute-start | bytes 786440 | tf_op jit(solution)/shard_map/ppermute | solution.py:12
  163.0 21.0 %collective-permute-start.13 = (bf16[1024,1,128]{2,0,1:T(8,128)(2,1)}, bf16[1024,1,128]{2,0,1:T(8,128)(2,1)}, u32[]{:S(2)}, u32[]{:S(2)}) collective-permute-start(bf16[1024,1,128]{2,0,1:T(8,128)(2,1)} %collective-permute-done.8), channel_id=1, source_target_pairs={{0,16},{1,17},{2,18},{3,19},{4,20},{5,21},{6,22},{7,23},{8,24},{9,... | collective-permute-start | bytes 786440 | tf_op jit(solution)/shard_map/ppermute | solution.py:12
  202.8 15.3 %copy-start.15 = (f32[2,512,1,128]{3,1,2,0:T(8,128)S(1)}, f32[2,512,1,128]{3,1,2,0:T(8,128)}, u32[]{:S(2)}) copy-start(f32[2,512,1,128]{3,1,2,0:T(8,128)} %get-tuple-element.267) | copy-start | bytes 1572868
  202.8 15.3 %copy-start.20 = (f32[2,512,1,128]{3,1,2,0:T(8,128)S(1)}, f32[2,512,1,128]{3,1,2,0:T(8,128)}, u32[]{:S(2)}) copy-start(f32[2,512,1,128]{3,1,2,0:T(8,128)} %get-tuple-element.268) | copy-start | bytes 1572868
  202.9 15.3 %copy-start.25 = (f32[2,512,1,128]{3,1,2,0:T(8,128)S(1)}, f32[2,512,1,128]{3,1,2,0:T(8,128)}, u32[]{:S(2)}) copy-start(f32[2,512,1,128]{3,1,2,0:T(8,128)} %get-tuple-element.269) | copy-start | bytes 1572868
  205.3 19.7 %all-to-all-start.6 = ((bf16[8,128,128]{2,1,0:T(8,128)(2,1)}), bf16[8,128,128]{2,1,0:T(8,128)(2,1)S(1)}, u32[]{:S(2)}, u32[]{:S(2)}) async-start(bf16[8,128,128]{2,1,0:T(8,128)(2,1)} %bitcast.26), calls=%async_computation.6 | async-start | bytes 524288 | tf_op jit(solution)/shard_map/all_to_all | solution.py:145
  212.4 19.7 %copy-start.5 = (f32[1024,1,128]{0,2,1:T(8,128)S(1)}, f32[1024,1,128]{0,2,1:T(8,128)}, u32[]{:S(2)}) copy-start(f32[1024,1,128]{0,2,1:T(8,128)} %get-tuple-element.262) | copy-start | bytes 1572868
  214.4 17.8 %collective-permute-start.10 = (f32[1024,1,128]{0,2,1:T(8,128)}, f32[1024,1,128]{0,2,1:T(8,128)}, u32[]{:S(2)}, u32[]{:S(2)}) collective-permute-start(f32[1024,1,128]{0,2,1:T(8,128)} %add.120), channel_id=1, source_target_pairs={{0,16},{1,17},{2,18},{3,19},{4,20},{5,21},{6,22},{7,23},{8,24},{9,... | collective-permute-start | bytes 1572872 | tf_op jit(solution)/shard_map/ppermute | solution.py:12
  225.1 20.1 %all-to-all-start.7 = ((bf16[8,128,128]{2,1,0:T(8,128)(2,1)}), bf16[8,128,128]{2,1,0:T(8,128)(2,1)S(1)}, u32[]{:S(2)}, u32[]{:S(2)}) async-start(bf16[8,128,128]{2,1,0:T(8,128)(2,1)} %bitcast.29), calls=%async_computation.7 | async-start | bytes 524288 | tf_op jit(solution)/shard_map/all_to_all | solution.py:146
  233.3 11.1 %collective-permute-start.15 = (bf16[1024,1,128]{0,2,1:T(8,128)(2,1)S(1)}, bf16[1024,1,128]{0,2,1:T(8,128)(2,1)S(1)}, u32[]{:S(2)}, u32[]{:S(2)}) collective-permute-start(bf16[1024,1,128]{0,2,1:T(8,128)(2,1)S(1)} %add.123), channel_id=1, source_target_pairs={{0,16},{1,17},{2,18},{3,19},{4,20},{5,21},{6,22},{7,23},{8,24},{9,... | collective-permute-start | bytes 786440 | tf_op jit(solution)/shard_map/ppermute | solution.py:12
  245.2 19.1 %all-to-all-start.5 = ((bf16[8,128,128]{2,1,0:T(8,128)(2,1)}), bf16[8,128,128]{2,1,0:T(8,128)(2,1)S(1)}, u32[]{:S(2)}, u32[]{:S(2)}) async-start(bf16[8,128,128]{2,1,0:T(8,128)(2,1)} %bitcast.23), calls=%async_computation.5 | async-start | bytes 524288 | tf_op jit(solution)/shard_map/all_to_all | solution.py:144
  (42 other events, 96.0 us)
where the time goes:
time: 268 us; the launch traced here: 265 us
  starting transfers between devices  89.2 us (33%)
  waiting for transfers between devices  77.7 us (29%)
  matrix products  61.2 us (23%)
  local copies, waits for them, and re-layouts  26.9 us (10%)
  other arithmetic  8.48 us (3%)
    ppermute x16, starting transfers between devices, passed_along(): return lax.ppermute(value, axis, pairs)  48.3 us
    ppermute x16, waiting for transfers between devices, passed_along(): return lax.ppermute(value, axis, pairs)  15.8 us
    dot_general x8, matrix products, tile_grads(): jnp.einsum('hqk,khd->qhd', grad_scores, key_tile, preferred_element_type=...  13.8 us
    dot_general x8, matrix products, tile_grads(): jnp.einsum('qhd,khd->hqk', query_tile, key_tile, preferred_element_type=j...  12.7 us
    dot_general x8, matrix products, tile_grads(): jnp.einsum('hqk,qhd->khd', probs_low, cotangent_tile, preferred_element_t...  12.6 us
    all_to_all x1, waiting for transfers between devices, per_device(): lax.all_to_all(grad_output, 'ulysses', split_axis=1, concat_axis=0, tiled...  11.7 us
    all_to_all x1, waiting for transfers between devices, per_device(): lax.all_to_all(attn_output, 'ulysses', split_axis=1, concat_axis=0, tiled...  11.3 us
    all_to_all x1, waiting for transfers between devices, per_device(): lax.all_to_all(queries, 'ulysses', split_axis=1, concat_axis=0, tiled=True)  11.2 us
  transfers between devices with their start and end apart: 24, of which 10 were waited for; matrix products, arithmetic and copies ran while one was open for 33% of the time, Pallas kernels for 0%

commit v1 on v0

v1 whole, which is shorter than its diff:
```python
import functools

import jax
import jax.numpy as jnp
from jax import lax
from jax.experimental import pallas as pl
from jax.experimental.pallas import tpu as pltpu
from jax.sharding import PartitionSpec as P

SPAN = 4
HEAD_DIM = 128
LOG2E = 1.4426950408889634
SCALE = HEAD_DIM ** -0.5
ROWS = 128
OWNERS = 8
HALF = OWNERS // 2
EXTRA = 16
TILE = 2
KTILE = 2
f32 = jnp.float32
bf16 = jnp.bfloat16
VMEM = pl.BlockSpec(memory_space=pltpu.VMEM)
SMEM = pl.BlockSpec(memory_space=pltpu.SMEM)
PARAMS = pltpu.CompilerParams(vmem_limit_bytes=48 * 1024 * 1024)


def three_terms(row):
    high = row.astype(bf16).astype(f32)
    rest = row - high
    middle = rest.astype(bf16).astype(f32)
    return (high, middle, rest - middle)


def pack_kernel(query_ref, key_ref, value_ref, output_ref, cotangent_ref, packed_ref):
    place = lax.broadcasted_iota(jnp.int32, (EXTRA, ROWS), 0)
    for head in range(OWNERS):
        columns = pl.ds(head * HEAD_DIM, HEAD_DIM)
        cotangent = cotangent_ref[:, columns]
        packed_ref[head, 0:128, :] = query_ref[:, columns]
        packed_ref[head, 128:256, :] = cotangent
        packed_ref[head, 256:384, :] = key_ref[:, columns]
        packed_ref[head, 384:512, :] = value_ref[:, columns]
        product = cotangent.astype(f32) * output_ref[:, columns].astype(f32)
        delta = jnp.sum(product.T, axis=0, keepdims=True)
        high, middle, low = three_terms(delta)
        rows = jnp.where(
            place == 0, high, jnp.where(place == 1, middle, jnp.where(place == 2, low, 0.0))
        )
        packed_ref[head, 512:528, :] = rows.astype(bf16)


def split_kernel(moved_ref, lse_ref, query_side_ref, key_side_ref):
    place = lax.broadcasted_iota(jnp.int32, (EXTRA, ROWS), 0)
    for owner in range(OWNERS):
        query_side_ref[owner, 0:256, :] = moved_ref[owner, 0:256, :]
        key_side_ref[owner] = moved_ref[owner, 256:512, :]
        high, middle, low = three_terms(lse_ref[owner : owner + 1, :])
        rows = moved_ref[owner, 512:528, :].astype(f32)
        rows = jnp.where(
            place == 3, high, jnp.where(place == 4, middle, jnp.where(place == 5, low, rows))
        )
        query_side_ref[owner, 256:272, :] = rows.astype(bf16)


def read_rows(query_side_ref, lse_ref, delta_ref):
    for owner in range(OWNERS):
        rows = query_side_ref[owner, 256:272, :].astype(f32)
        delta = rows[0:1] + rows[1:2] + rows[2:3]
        lse = rows[3:4] + rows[4:5] + rows[5:6]
        group, part = owner // TILE, owner % TILE
        delta_ref[group, :, part * ROWS : (part + 1) * ROWS] = delta
        lse_ref[group, :, part * ROWS : (part + 1) * ROWS] = lse * LOG2E


def nt(left, right):
    return lax.dot_general(left, right, (((1,), (1,)), ((), ())), preferred_element_type=f32)


def nn(left, right):
    return lax.dot_general(left, right, (((1,), (0,)), ((), ())), preferred_element_type=f32)


def tn(left, right):
    return lax.dot_general(left, right, (((0,), (0,)), ((), ())), preferred_element_type=f32)


def block_grads(query_half, key_half, query_refs, key_refs, diagonal):
    query_side_ref, lse_ref, delta_ref, grad_query_ref = query_refs
    key_side_ref, grad_key_ref, grad_value_ref = key_refs
    query_rows, key_rows = TILE * ROWS, KTILE * ROWS
    for key_tile in range(HALF // KTILE):
        keys_at = pl.ds(key_half * HALF + key_tile * KTILE, KTILE)
        key = key_side_ref[keys_at, 0:128, :].reshape(key_rows, HEAD_DIM)
        value = key_side_ref[keys_at, 128:256, :].reshape(key_rows, HEAD_DIM)
        grad_key = grad_key_ref[keys_at].reshape(key_rows, HEAD_DIM)
        grad_value = grad_value_ref[keys_at].reshape(key_rows, HEAD_DIM)
        for query_tile in range(HALF // TILE):
            first_query = query_tile * query_rows
            first_key = key_tile * key_rows
            if diagonal and first_query + query_rows <= first_key:
                continue
            queries_at = pl.ds(query_half * HALF + query_tile * TILE, TILE)
            group = query_half * (HALF // TILE) + query_tile
            query = query_side_ref[queries_at, 0:128, :].reshape(query_rows, HEAD_DIM)
            cotangent = query_side_ref[queries_at, 128:256, :].reshape(query_rows, HEAD_DIM)
            scores = nt(key, query)
            probs = jnp.exp2(scores * (SCALE * LOG2E) - lse_ref[group])
            if diagonal and first_query < first_key + key_rows - 1:
                key_place = first_key + lax.broadcasted_iota(jnp.int32, probs.shape, 0)
                query_place = first_query + lax.broadcasted_iota(jnp.int32, probs.shape, 1)
                probs = jnp.where(query_place >= key_place, probs, 0.0)
            grad_probs = nt(value, cotangent)
            grad_scores = (probs * (grad_probs - delta_ref[group])).astype(bf16)
            grad_value += nn(probs.astype(bf16), cotangent)
            grad_key += nn(grad_scores, query)
            grad_query = tn(grad_scores, key)
            grad_query_ref[queries_at] += grad_query.reshape(TILE, ROWS, HEAD_DIM)
        grad_key_ref[keys_at] = grad_key.reshape(KTILE, ROWS, HEAD_DIM)
        grad_value_ref[keys_at] = grad_value.reshape(KTILE, ROWS, HEAD_DIM)


def own_kernel(
    query_side_ref, key_side_ref, grad_query_ref, grad_key_ref, grad_value_ref, lse_ref, delta_ref
):
    grad_query_ref[...] = jnp.zeros_like(grad_query_ref)
    grad_key_ref[...] = jnp.zeros_like(grad_key_ref)
    grad_value_ref[...] = jnp.zeros_like(grad_value_ref)
    read_rows(query_side_ref, lse_ref, delta_ref)
    query_refs = (query_side_ref, lse_ref, delta_ref, grad_query_ref)
    key_refs = (key_side_ref, grad_key_ref, grad_value_ref)
    block_grads(1, 0, query_refs, key_refs, False)
    block_grads(0, 0, query_refs, key_refs, True)
    block_grads(1, 1, query_refs, key_refs, True)


def cross_kernel(
    halves_ref,
    query_side_ref,
    key_side_ref,
    far_query_side_ref,
    far_key_side_ref,
    first_query_ref,
    first_key_ref,
    first_value_ref,
    grad_query_ref,
    grad_key_ref,
    grad_value_ref,
    far_grad_query_ref,
    far_grad_pair_ref,
    lse_ref,
    delta_ref,
    far_lse_ref,
    far_delta_ref,
    far_query_sum,
    far_key_sum,
    far_value_sum,
):
    grad_query_ref[...] = first_query_ref[...]
    grad_key_ref[...] = first_key_ref[...]
    grad_value_ref[...] = first_value_ref[...]
    far_query_sum[...] = jnp.zeros_like(far_query_sum)
    far_key_sum[...] = jnp.zeros_like(far_key_sum)
    far_value_sum[...] = jnp.zeros_like(far_value_sum)
    read_rows(query_side_ref, lse_ref, delta_ref)
    read_rows(far_query_side_ref, far_lse_ref, far_delta_ref)
    near_query = (query_side_ref, lse_ref, delta_ref, grad_query_ref)
    far_query = (far_query_side_ref, far_lse_ref, far_delta_ref, far_query_sum)
    near_key = (key_side_ref, grad_key_ref, grad_value_ref)
    far_key = (far_key_side_ref, far_key_sum, far_value_sum)
    for index, (query_refs, key_refs) in enumerate(
        ((far_query, far_key), (near_query, far_key), (far_query, near_key))
    ):
        half = halves_ref[index]
        block_grads(1, 0, query_refs, key_refs, False)
        block_grads(half, half, query_refs, key_refs, False)
    grad_query_ref[...] = grad_query_ref[...] * SCALE
    grad_key_ref[...] = grad_key_ref[...] * SCALE
    far_grad_query_ref[...] = (far_query_sum[...] * SCALE).astype(bf16)
    far_grad_pair_ref[0] = (far_key_sum[...] * SCALE).astype(bf16)
    far_grad_pair_ref[1] = far_value_sum[...].astype(bf16)


def join_kernel(
    grad_query_ref, grad_key_ref, grad_value_ref, back_query_ref, back_pair_ref, packed_ref
):
    packed_ref[:, 0:128, :] = (grad_query_ref[...] + back_query_ref[...].astype(f32)).astype(bf16)
    packed_ref[:, 128:256, :] = (grad_key_ref[...] + back_pair_ref[0].astype(f32)).astype(bf16)
    packed_ref[:, 256:384, :] = (grad_value_ref[...] + back_pair_ref[1].astype(f32)).astype(bf16)


def unpack_kernel(moved_ref, grad_query_ref, grad_key_ref, grad_value_ref):
    for head in range(OWNERS):
        columns = pl.ds(head * HEAD_DIM, HEAD_DIM)
        grad_query_ref[:, columns] = moved_ref[head, 0:128, :]
        grad_key_ref[:, columns] = moved_ref[head, 128:256, :]
        grad_value_ref[:, columns] = moved_ref[head, 256:384, :]


def call(kernel, args, specs, outs, scratch=(), flops=0, moved=4 << 20, name=None):
    return pl.pallas_call(
        kernel,
        out_shape=[jax.ShapeDtypeStruct(shape, dtype) for shape, dtype in outs],
        in_specs=specs,
        out_specs=[VMEM] * len(outs),
        scratch_shapes=list(scratch),
        compiler_params=PARAMS,
        cost_estimate=pl.CostEstimate(flops=flops, bytes_accessed=moved, transcendentals=0),
        name=name,
    )(*args)


def row_scratch():
    return pltpu.VMEM((OWNERS // TILE, 1, TILE * ROWS), f32)


def per_device(queries, key_rows, value_rows, attn_output, grad_output, logsumexp, positions):
    blk_count = lax.axis_size("blk")
    stride = blk_count // SPAN
    run_rows = logsumexp.shape[0]
    here = lax.axis_index("blk")
    place, line = here // stride, here % stride
    query_mate = lambda at: at ^ 1
    key_mate = lambda at: SPAN - 1 - at

    def swapped(value, mate):
        pairs = [(b, mate(b // stride) * stride + b % stride) for b in range(blk_count)]
        return lax.ppermute(value, "blk", pairs)

    def first_place(at):
        start = (at * stride + line) * run_rows
        return lax.dynamic_slice_in_dim(positions, start, 1)

    own_first = first_place(place)
    query_first = first_place(query_mate(place))
    key_first = first_place(key_mate(place))
    halves = jnp.concatenate(
        [query_first < key_first, own_first < key_first, query_first < own_first]
    ).astype(jnp.int32)

    side = (OWNERS, ROWS, HEAD_DIM)
    (packed,) = call(
        pack_kernel,
        (queries, key_rows, value_rows, attn_output, grad_output),
        [VMEM] * 5,
        [((OWNERS, 528, HEAD_DIM), bf16)],
        name="pack",
    )
    moved = lax.all_to_all(packed, "ulysses", split_axis=0, concat_axis=0, tiled=True)
    query_side, key_side = call(
        split_kernel,
        (moved, logsumexp.reshape(OWNERS, ROWS)),
        [VMEM] * 2,
        [((OWNERS, 272, HEAD_DIM), bf16), ((OWNERS, 256, HEAD_DIM), bf16)],
        name="split",
    )
    far_query_side = swapped(query_side, query_mate)
    far_key_side = swapped(key_side, key_mate)
    own = call(
        own_kernel,
        (query_side, key_side),
        [VMEM] * 2,
        [(side, f32)] * 3,
        [row_scratch(), row_scratch()],
        flops=10 * 128 * 10 * 256 * 256,
        name="own",
    )
    grad_query, grad_key, grad_value, far_grad_query, far_grad_pair = call(
        cross_kernel,
        (halves, query_side, key_side, far_query_side, far_key_side, *own),
        [SMEM] + [VMEM] * 7,
        [(side, f32)] * 3 + [(side, bf16), ((2,) + side, bf16)],
        [row_scratch() for _ in range(4)] + [pltpu.VMEM(side, f32) for _ in range(3)],
        flops=10 * 128 * 24 * 256 * 256,
        name="cross",
    )
    back_query = swapped(far_grad_query, query_mate)
    back_pair = swapped(far_grad_pair, key_mate)
    (joined,) = call(
        join_kernel,
        (grad_query, grad_key, grad_value, back_query, back_pair),
        [VMEM] * 5,
        [((OWNERS, 384, HEAD_DIM), bf16)],
        name="join",
    )
    returned = lax.all_to_all(joined, "ulysses", split_axis=0, concat_axis=0, tiled=True)
    return tuple(
        call(
            unpack_kernel,
            (returned,),
            [VMEM],
            [((ROWS, OWNERS * HEAD_DIM), bf16)] * 3,
            name="unpack",
        )
    )


def solution(mesh):
    tokens = P(("blk", "ulysses"), None)
    return jax.shard_map(
        per_device,
        mesh=mesh,
        in_specs=(tokens,) * 5 + (P("blk", "ulysses"), P()),
        out_specs=(tokens,) * 3,
        check_vma=False,
    )
```

time: 268 us -> 118 us (0.44)
  starting transfers between devices: 89.2 us -> 13.3 us
  blocking collectives: 0 us -> 66.6 us
  waiting for transfers between devices: 77.7 us -> 13.5 us
  matrix products: 61.2 us -> 0 us
  local copies, waits for them, and re-layouts: 26.9 us -> 6.07 us
  Pallas kernels: 0 us -> 12.8 us
  other arithmetic: 8.48 us -> 0.08 us
  between operations: 1.12 us -> 4.64 us
    all_to_all x0 -> x2, blocking collectives: none -> 66.6 us  [the longest x1 40.4 us: per_device(): lax.all_to_all(packed, 'ulysses', split_axis=0, concat_axis=0, tiled=True)]
    all_to_all x8 -> x0, waiting for transfers between devices: 61.9 us -> none  [the longest x1 11.7 us: per_device(): lax.all_to_all(grad_output, 'ulysses', split_axis=1, concat_axis=0, tiled...]
    dot_general x40 -> x0, matrix products: 61.2 us -> none  [the longest x8 13.8 us: tile_grads(): jnp.einsum('hqk,khd->qhd', grad_scores, key_tile, preferred_element_type=...]
    all_to_all x8 -> x0, starting transfers between devices: 40.9 us -> none  [the longest x1 10.3 us: per_device(): lax.all_to_all(key_rows, 'ulysses', split_axis=1, concat_axis=0, tiled=True)]
    ppermute x16 -> x4, starting transfers between devices: 48.3 us -> 13.3 us  [swapped(): return lax.ppermute(value, 'blk', pairs)]
    pallas_call x0 -> x6, Pallas kernels: none -> 12.8 us  [call(): pl.pallas_call(kernel, out_shape=[jax.ShapeDtypeStruct(shape, dtype) for...]
    another operation x8 -> x0, local copies, waits for them, and re-layouts: 6.7 us -> none
    while x80 -> x0, local copies, waits for them, and re-layouts: 6.44 us -> none
  transfers between devices with their start and end apart: 24 -> 4, of which waited for: 10 -> 3; matrix products, arithmetic and copies ran while one was open for 33% -> 1% of each run, Pallas kernels for 0% -> 3%
where the time goes in v1:
time: 118 us; the launch traced here: 117 us
  blocking collectives  66.6 us (56%)
  waiting for transfers between devices  13.5 us (11%)
  starting transfers between devices  13.3 us (11%)
  Pallas kernels  12.8 us (11%)
  local copies, waits for them, and re-layouts  6.07 us (5%)
  between operations  4.64 us (4%)
    all_to_all x1, blocking collectives, per_device(): lax.all_to_all(packed, 'ulysses', split_axis=0, concat_axis=0, tiled=True)  40.4 us
    all_to_all x1, blocking collectives, per_device(): lax.all_to_all(joined, 'ulysses', split_axis=0, concat_axis=0, tiled=True)  26.2 us
    ppermute x4, waiting for transfers between devices, swapped(): return lax.ppermute(value, 'blk', pairs)  13.5 us
    ppermute x4, starting transfers between devices, swapped(): return lax.ppermute(value, 'blk', pairs)  13.3 us
    pallas_call x6, Pallas kernels, call(): pl.pallas_call(kernel, out_shape=[jax.ShapeDtypeStruct(shape, dtype) for...  12.8 us
    unnamed x12, local copies, waits for them, and re-layouts  4.75 us
  transfers between devices with their start and end apart: 4, of which 3 were waited for; matrix products, arithmetic and copies ran while one was open for 1% of the time, Pallas kernels for 3%

profile of v1, /device:TPU:56, one launch (start us, length us, event | category | flops | bytes accessed | tf_op | source)
XLA Modules:
  0.0 117.0 jit_solution(9184576232249362467)
XLA Ops:
  0.6 0.0 copy-start
  0.6 0.9 copy-done
  1.6 0.0 copy-start.1
  1.6 0.9 copy-done.1
  2.5 0.0 copy-start.2
  2.5 0.9 copy-done.2
  3.5 0.0 copy-start.3
  3.5 0.9 copy-done.3
  4.4 0.0 copy-start.4
  4.4 0.9 copy-done.4
  5.4 0.3 pack.1
  5.7 0.0 copy-start.5
  5.7 40.4 %all_to_all.10.moved_ref = bf16[8,528,128]{2,1,0:T(8,128)(2,1)S(1)} all-to-all(bf16[8,528,128]{2,1,0:T(8,128)(2,1)S(1)} %pack.1), channel_id=1, replica_groups=mesh['ulysses'=8,'blk'=64] {'ulysses'}, dimensions={0} | all-to-all | bytes 2162688 | tf_op jit(solution)/shard_map/all_to_all | solution.py:248
  46.1 0.0 copy-done.5
  46.1 0.1 split.1
  46.2 3.4 %collective-permute-start = (bf16[8,272,128]{2,1,0:T(8,128)(2,1)S(1)}, bf16[8,272,128]{2,1,0:T(8,128)(2,1)S(1)}, u32[]{:S(2)}, u32[]{:S(2)}) collective-permute-start(bf16[8,272,128]{2,1,0:T(8,128)(2,1)S(1)} %get-tuple-element.13.query_side_ref), channel_id=1, source_target_pairs={{0,16},{1,17},{2,18},{3,19},{4,20},{5,21},{6,22},{7,23},{8,24},{9,... | collective-permute-start | bytes 1671176 | tf_op jit(solution)/shard_map/ppermute | solution.py:227
  49.6 4.0 %collective-permute-start.1 = (bf16[8,256,128]{2,1,0:T(8,128)(2,1)S(1)}, bf16[8,256,128]{2,1,0:T(8,128)(2,1)S(1)}, u32[]{:S(2)}, u32[]{:S(2)}) collective-permute-start(bf16[8,256,128]{2,1,0:T(8,128)(2,1)S(1)} %get-tuple-element.14.key_side_ref), channel_id=1, source_target_pairs={{0,48},{1,49},{2,50},{3,51},{4,52},{5,53},{6,54},{7,55},{8,56},{9,... | collective-permute-start | bytes 1572872 | tf_op jit(solution)/shard_map/ppermute | solution.py:227
  53.7 1.3 %fusion = (s32[1]{0:T(128)}, s32[1]{0:T(128)}, s32[1]{0:T(128)}) fusion(s32[65536]{0:T(1024)} %param.13, s32[]{:T(128)S(6)} %select_n.23, s32[]{:T(128)S(6)} %select_n.22, s32[]{:T(128)S(6)} %select_n.24), kind=kLoop, calls=%fused_computation.1 | loop fusion | bytes 36 | tf_op jit(solution)/shard_map/dynamic_slice | solution.py:231
  58.9 0.1 add_convert_fusion.halves_ref
  59.0 3.2 %own.1 = (f32[8,128,128]{2,1,0:T(8,128)S(1)}, f32[8,128,128]{2,1,0:T(8,128)S(1)}, f32[8,128,128]{2,1,0:T(8,128)S(1)}) custom-call(bf16[8,272,128]{2,1,0:T(8,128)(2,1)S(1)} %get-tuple-element.13.query_side_ref, bf16[8,256,128]{2,1,0:T(8,128)(2,1)S(1)} %get-tuple-element.14.key_side_ref), custom_call_target="tpu_custom_call" | custom-call | flops 838860800 | bytes 4194304 | tf_op jit(solution)/shard_map/own/pallas_call | solution.py:200
  62.2 3.9 %collective-permute-done.1.far_key_side_ref = bf16[8,256,128]{2,1,0:T(8,128)(2,1)S(1)} collective-permute-done((bf16[8,256,128]{2,1,0:T(8,128)(2,1)S(1)}, bf16[8,256,128]{2,1,0:T(8,128)(2,1)S(1)}, u32[]{:S(2)}, u32[]{:S(2)}) %collective-permute-start.1) | collective-permute-done | bytes 524320 | tf_op jit(solution)/shard_map/ppermute | solution.py:227
  66.0 0.0 collective-permute-done.far_query_side_ref
  66.1 8.0 %cross.1 = (f32[8,128,128]{2,1,0:T(8,128)S(1)}, f32[8,128,128]{2,1,0:T(8,128)S(1)}, f32[8,128,128]{2,1,0:T(8,128)S(1)}, bf16[8,128,128]{2,1,0:T(8,128)(2,1)S(1)}, bf16[2,8,128,128]{3,2,1,0:T(8,128)(2,1)S(1)}) custom-call(s32[3]{0:T(128)S(1)} %add_convert_fusion.halves_ref, bf16[8,272,128]{2,1,0:T(8,128)(2,1)S(1)} %get-tuple-element.13.query_side_ref, ...), custom_call_target="tpu_custom_call" | custom-call | flops 2013265920 | bytes 4194304 | tf_op jit(solution)/shard_map/cross/pallas_call | solution.py:200
  74.1 4.0 %collective-permute-start.3 = (bf16[2,8,128,128]{3,2,1,0:T(8,128)(2,1)S(1)}, bf16[2,8,128,128]{3,2,1,0:T(8,128)(2,1)S(1)}, u32[]{:S(2)}, u32[]{:S(2)}) collective-permute-start(bf16[2,8,128,128]{3,2,1,0:T(8,128)(2,1)S(1)} %get-tuple-element.22), channel_id=1, source_target_pairs={{0,48},{1,49},{2,50},{3,51},{4,52},{5,53},{6,54},{7,55},{8,56},{9,... | collective-permute-start | bytes 1572872 | tf_op jit(solution)/shard_map/ppermute | solution.py:227
  78.1 1.9 %collective-permute-start.2 = (bf16[8,128,128]{2,1,0:T(8,128)(2,1)S(1)}, bf16[8,128,128]{2,1,0:T(8,128)(2,1)S(1)}, u32[]{:S(2)}, u32[]{:S(2)}) collective-permute-start(bf16[8,128,128]{2,1,0:T(8,128)(2,1)S(1)} %get-tuple-element.21), channel_id=1, source_target_pairs={{0,16},{1,17},{2,18},{3,19},{4,20},{5,21},{6,22},{7,23},{8,24},{9,... | collective-permute-start | bytes 786440 | tf_op jit(solution)/shard_map/ppermute | solution.py:227
  80.0 6.5 %collective-permute-done.2.back_query_ref = bf16[8,128,128]{2,1,0:T(8,128)(2,1)S(1)} collective-permute-done((bf16[8,128,128]{2,1,0:T(8,128)(2,1)S(1)}, bf16[8,128,128]{2,1,0:T(8,128)(2,1)S(1)}, u32[]{:S(2)}, u32[]{:S(2)}) %collective-permute-start.2) | collective-permute-done | bytes 262176 | tf_op jit(solution)/shard_map/ppermute | solution.py:227
  86.5 3.1 %collective-permute-done.3.back_pair_ref = bf16[2,8,128,128]{3,2,1,0:T(8,128)(2,1)S(1)} collective-permute-done((bf16[2,8,128,128]{3,2,1,0:T(8,128)(2,1)S(1)}, bf16[2,8,128,128]{3,2,1,0:T(8,128)(2,1)S(1)}, u32[]{:S(2)}, u32[]{:S(2)}) %collective-permute-start.3) | collective-permute-done | bytes 524320 | tf_op jit(solution)/shard_map/ppermute | solution.py:227
  89.6 0.2 join.1
  89.7 26.2 %all_to_all.11.moved_ref = bf16[8,384,128]{2,1,0:T(8,128)(2,1)S(1)} all-to-all(bf16[8,384,128]{2,1,0:T(8,128)(2,1)S(1)} %join.1), channel_id=1, replica_groups=mesh['ulysses'=8,'blk'=64] {'ulysses'}, dimensions={0} | all-to-all | bytes 1572864 | tf_op jit(solution)/shard_map/all_to_all | solution.py:285
  115.9 1.1 unpack.1
Async XLA Ops:
  0.6 1.0 copy-start
  1.6 0.9 copy-start.1
  2.5 0.9 copy-start.2
  3.5 0.9 copy-start.3
  4.4 0.9 copy-start.4
  5.7 40.5 %copy-start.5 = (f32[1024,1]{0,1:T(1,128)S(1)}, f32[1024,1]{0,1:T(1,128)}, u32[]{:S(2)}) copy-start(f32[1024,1]{0,1:T(1,128)} %param.12) | copy-start | bytes 12292
  46.2 19.8 %collective-permute-start = (bf16[8,272,128]{2,1,0:T(8,128)(2,1)S(1)}, bf16[8,272,128]{2,1,0:T(8,128)(2,1)S(1)}, u32[]{:S(2)}, u32[]{:S(2)}) collective-permute-start(bf16[8,272,128]{2,1,0:T(8,128)(2,1)S(1)} %get-tuple-element.13.query_side_ref), channel_id=1, source_target_pairs={{0,16},{1,17},{2,18},{3,19},{4,20},{5,21},{6,22},{7,23},{8,24},{9,... | collective-permute-start | bytes 1671176 | tf_op jit(solution)/shard_map/ppermute | solution.py:227
  49.6 16.4 %collective-permute-start.1 = (bf16[8,256,128]{2,1,0:T(8,128)(2,1)S(1)}, bf16[8,256,128]{2,1,0:T(8,128)(2,1)S(1)}, u32[]{:S(2)}, u32[]{:S(2)}) collective-permute-start(bf16[8,256,128]{2,1,0:T(8,128)(2,1)S(1)} %get-tuple-element.14.key_side_ref), channel_id=1, source_target_pairs={{0,48},{1,49},{2,50},{3,51},{4,52},{5,53},{6,54},{7,55},{8,56},{9,... | collective-permute-start | bytes 1572872 | tf_op jit(solution)/shard_map/ppermute | solution.py:227
  74.1 15.5 %collective-permute-start.3 = (bf16[2,8,128,128]{3,2,1,0:T(8,128)(2,1)S(1)}, bf16[2,8,128,128]{3,2,1,0:T(8,128)(2,1)S(1)}, u32[]{:S(2)}, u32[]{:S(2)}) collective-permute-start(bf16[2,8,128,128]{3,2,1,0:T(8,128)(2,1)S(1)} %get-tuple-element.22), channel_id=1, source_target_pairs={{0,48},{1,49},{2,50},{3,51},{4,52},{5,53},{6,54},{7,55},{8,56},{9,... | collective-permute-start | bytes 1572872 | tf_op jit(solution)/shard_map/ppermute | solution.py:227
  78.1 8.4 %collective-permute-start.2 = (bf16[8,128,128]{2,1,0:T(8,128)(2,1)S(1)}, bf16[8,128,128]{2,1,0:T(8,128)(2,1)S(1)}, u32[]{:S(2)}, u32[]{:S(2)}) collective-permute-start(bf16[8,128,128]{2,1,0:T(8,128)(2,1)S(1)} %get-tuple-element.21), channel_id=1, source_target_pairs={{0,16},{1,17},{2,18},{3,19},{4,20},{5,21},{6,22},{7,23},{8,24},{9,... | collective-permute-start | bytes 786440 | tf_op jit(solution)/shard_map/ppermute | solution.py:227

commit v2 on v1

--- a/solution.py
+++ b/solution.py
@@ -20,6 +20,7 @@
 f32 = jnp.float32
 bf16 = jnp.bfloat16
 VMEM = pl.BlockSpec(memory_space=pltpu.VMEM)
+HBM = pl.BlockSpec(memory_space=pltpu.HBM)
 SMEM = pl.BlockSpec(memory_space=pltpu.SMEM)
 PARAMS = pltpu.CompilerParams(vmem_limit_bytes=48 * 1024 * 1024)
 
@@ -31,22 +32,36 @@
     return (high, middle, rest - middle)
 
 
-def pack_kernel(query_ref, key_ref, value_ref, output_ref, cotangent_ref, packed_ref):
+def pack_kernel(
+    query_ref, key_ref, value_ref, output_ref, cotangent_ref, packed_ref, output_here, arrived
+):
+    def copies(index, source):
+        for head in range(OWNERS):
+            columns = pl.ds(head * HEAD_DIM, HEAD_DIM)
+            target = output_here.at[head]
+            if index < 4:
+                target = packed_ref.at[head, pl.ds(index * ROWS, ROWS), :]
+            yield pltpu.make_async_copy(source.at[:, columns], target, arrived.at[index, head])
+
+    sources = (query_ref, cotangent_ref, key_ref, value_ref, output_ref)
+    moves = [list(copies(index, source)) for index, source in enumerate(sources)]
+    for index in (1, 4, 0, 2, 3):
+        for move in moves[index]:
+            move.start()
     place = lax.broadcasted_iota(jnp.int32, (EXTRA, ROWS), 0)
     for head in range(OWNERS):
-        columns = pl.ds(head * HEAD_DIM, HEAD_DIM)
-        cotangent = cotangent_ref[:, columns]
-        packed_ref[head, 0:128, :] = query_ref[:, columns]
-        packed_ref[head, 128:256, :] = cotangent
-        packed_ref[head, 256:384, :] = key_ref[:, columns]
-        packed_ref[head, 384:512, :] = value_ref[:, columns]
-        product = cotangent.astype(f32) * output_ref[:, columns].astype(f32)
+        moves[1][head].wait()
+        moves[4][head].wait()
+        product = packed_ref[head, 128:256, :].astype(f32) * output_here[head].astype(f32)
         delta = jnp.sum(product.T, axis=0, keepdims=True)
         high, middle, low = three_terms(delta)
         rows = jnp.where(
             place == 0, high, jnp.where(place == 1, middle, jnp.where(place == 2, low, 0.0))
         )
         packed_ref[head, 512:528, :] = rows.astype(bf16)
+    for index in (0, 2, 3):
+        for move in moves[index]:
+            move.wait()
 
 
 def split_kernel(moved_ref, lse_ref, query_side_ref, key_side_ref):
@@ -133,51 +148,76 @@
     block_grads(1, 1, query_refs, key_refs, True)
 
 
-def cross_kernel(
+def pair_grads(half, query_refs, key_refs):
+    block_grads(1, 0, query_refs, key_refs, False)
+    block_grads(half, half, query_refs, key_refs, False)
+
+
+def near_far_kernel(
     halves_ref,
     query_side_ref,
-    key_side_ref,
+    far_key_side_ref,
+    first_query_ref,
+    grad_query_ref,
+    far_key_ref,
+    far_value_ref,
+    lse_ref,
+    delta_ref,
+):
+    grad_query_ref[...] = first_query_ref[...]
+    far_key_ref[...] = jnp.zeros_like(far_key_ref)
+    far_value_ref[...] = jnp.zeros_like(far_value_ref)
+    read_rows(query_side_ref, lse_ref, delta_ref)
+    near_query = (query_side_ref, lse_ref, delta_ref, grad_query_ref)
+    pair_grads(halves_ref[1], near_query, (far_key_side_ref, far_key_ref, far_value_ref))
+    grad_query_ref[...] = grad_query_ref[...] * SCALE
+
+
+def far_far_kernel(
+    halves_ref,
     far_query_side_ref,
     far_key_side_ref,
+    first_key_ref,
+    first_value_ref,
+    far_query_ref,
+    far_pair_ref,
+    lse_ref,
+    delta_ref,
+    far_key_sum,
+    far_value_sum,
+):
+    far_query_ref[...] = jnp.zeros_like(far_query_ref)
+    far_key_sum[...] = first_key_ref[...]
+    far_value_sum[...] = first_value_ref[...]
+    read_rows(far_query_side_ref, lse_ref, delta_ref)
+    far_query = (far_query_side_ref, lse_ref, delta_ref, far_query_ref)
+    pair_grads(halves_ref[0], far_query, (far_key_side_ref, far_key_sum, far_value_sum))
+    far_pair_ref[0] = (far_key_sum[...] * SCALE).astype(bf16)
+    far_pair_ref[1] = far_value_sum[...].astype(bf16)
+
+
+def far_near_kernel(
+    halves_ref,
+    far_query_side_ref,
+    key_side_ref,
     first_query_ref,
     first_key_ref,
     first_value_ref,
-    grad_query_ref,
+    far_query_ref,
     grad_key_ref,
     grad_value_ref,
-    far_grad_query_ref,
-    far_grad_pair_ref,
     lse_ref,
     delta_ref,
-    far_lse_ref,
-    far_delta_ref,
     far_query_sum,
-    far_key_sum,
-    far_value_sum,
-):
-    grad_query_ref[...] = first_query_ref[...]
+):
+    far_query_sum[...] = first_query_ref[...]
     grad_key_ref[...] = first_key_ref[...]
     grad_value_ref[...] = first_value_ref[...]
-    far_query_sum[...] = jnp.zeros_like(far_query_sum)
-    far_key_sum[...] = jnp.zeros_like(far_key_sum)
-    far_value_sum[...] = jnp.zeros_like(far_value_sum)
-    read_rows(query_side_ref, lse_ref, delta_ref)
-    read_rows(far_query_side_ref, far_lse_ref, far_delta_ref)
-    near_query = (query_side_ref, lse_ref, delta_ref, grad_query_ref)
-    far_query = (far_query_side_ref, far_lse_ref, far_delta_ref, far_query_sum)
-    near_key = (key_side_ref, grad_key_ref, grad_value_ref)
-    far_key = (far_key_side_ref, far_key_sum, far_value_sum)
-    for index, (query_refs, key_refs) in enumerate(
-        ((far_query, far_key), (near_query, far_key), (far_query, near_key))
-    ):
-        half = halves_ref[index]
-        block_grads(1, 0, query_refs, key_refs, False)
-        block_grads(half, half, query_refs, key_refs, False)
-    grad_query_ref[...] = grad_query_ref[...] * SCALE
+    read_rows(far_query_side_ref, lse_ref, delta_ref)
+    far_query = (far_query_side_ref, lse_ref, delta_ref, far_query_sum)
+    pair_grads(halves_ref[2], far_query, (key_side_ref, grad_key_ref, grad_value_ref))
     grad_key_ref[...] = grad_key_ref[...] * SCALE
-    far_grad_query_ref[...] = (far_query_sum[...] * SCALE).astype(bf16)
-    far_grad_pair_ref[0] = (far_key_sum[...] * SCALE).astype(bf16)
-    far_grad_pair_ref[1] = far_value_sum[...].astype(bf16)
+    far_query_ref[...] = (far_query_sum[...] * SCALE).astype(bf16)
 
 
 def join_kernel(
@@ -188,20 +228,27 @@
     packed_ref[:, 256:384, :] = (grad_value_ref[...] + back_pair_ref[1].astype(f32)).astype(bf16)
 
 
-def unpack_kernel(moved_ref, grad_query_ref, grad_key_ref, grad_value_ref):
+def unpack_kernel(moved_ref, grad_query_ref, grad_key_ref, grad_value_ref, sent):
+    moves = []
     for head in range(OWNERS):
         columns = pl.ds(head * HEAD_DIM, HEAD_DIM)
-        grad_query_ref[:, columns] = moved_ref[head, 0:128, :]
-        grad_key_ref[:, columns] = moved_ref[head, 128:256, :]
-        grad_value_ref[:, columns] = moved_ref[head, 256:384, :]
-
-
-def call(kernel, args, specs, outs, scratch=(), flops=0, moved=4 << 20, name=None):
+        for index, target in enumerate((grad_query_ref, grad_key_ref, grad_value_ref)):
+            source = moved_ref.at[head, pl.ds(index * ROWS, ROWS), :]
+            moves.append(
+                pltpu.make_async_copy(source, target.at[:, columns], sent.at[index, head])
+            )
+    for move in moves:
+        move.start()
+    for move in moves:
+        move.wait()
+
+
+def call(kernel, args, specs, outs, scratch=(), flops=0, moved=4 << 20, name=None, space=VMEM):
     return pl.pallas_call(
         kernel,
         out_shape=[jax.ShapeDtypeStruct(shape, dtype) for shape, dtype in outs],
         in_specs=specs,
-        out_specs=[VMEM] * len(outs),
+        out_specs=[space] * len(outs),
         scratch_shapes=list(scratch),
         compiler_params=PARAMS,
         cost_estimate=pl.CostEstimate(flops=flops, bytes_accessed=moved, transcendentals=0),
@@ -240,9 +287,10 @@
     side = (OWNERS, ROWS, HEAD_DIM)
     (packed,) = call(
         pack_kernel,
-        (queries, key_rows, value_rows, attn_output, grad_output),
-        [VMEM] * 5,
+        tuple(pltpu.with_memory_space_constraint(x, pltpu.HBM) for x in (queries, key_rows, value_rows, attn_output, grad_output)),
+        [HBM] * 5,
         [((OWNERS, 528, HEAD_DIM), bf16)],
+        [pltpu.VMEM((OWNERS, ROWS, HEAD_DIM), bf16), pltpu.SemaphoreType.DMA((5, OWNERS))],
         name="pack",
     )
     moved = lax.all_to_all(packed, "ulysses", split_axis=0, concat_axis=0, tiled=True)
@@ -253,8 +301,8 @@
         [((OWNERS, 272, HEAD_DIM), bf16), ((OWNERS, 256, HEAD_DIM), bf16)],
         name="split",
     )
+    far_key_side = swapped(key_side, key_mate)
     far_query_side = swapped(query_side, query_mate)
-    far_key_side = swapped(key_side, key_mate)
     own = call(
         own_kernel,
         (query_side, key_side),
@@ -264,17 +312,36 @@
         flops=10 * 128 * 10 * 256 * 256,
         name="own",
     )
-    grad_query, grad_key, grad_value, far_grad_query, far_grad_pair = call(
-        cross_kernel,
-        (halves, query_side, key_side, far_query_side, far_key_side, *own),
-        [SMEM] + [VMEM] * 7,
-        [(side, f32)] * 3 + [(side, bf16), ((2,) + side, bf16)],
-        [row_scratch() for _ in range(4)] + [pltpu.VMEM(side, f32) for _ in range(3)],
-        flops=10 * 128 * 24 * 256 * 256,
-        name="cross",
+    cost = 10 * 128 * 8 * 256 * 256
+    grad_query, first_far_key, first_far_value = call(
+        near_far_kernel,
+        (halves, query_side, far_key_side, own[0]),
+        [SMEM] + [VMEM] * 3,
+        [(side, f32)] * 3,
+        [row_scratch(), row_scratch()],
+        flops=cost,
+        name="near_far",
+    )
+    first_far_query, far_grad_pair = call(
+        far_far_kernel,
+        (halves, far_query_side, far_key_side, first_far_key, first_far_value),
+        [SMEM] + [VMEM] * 4,
+        [(side, f32), ((2,) + side, bf16)],
+        [row_scratch(), row_scratch(), pltpu.VMEM(side, f32), pltpu.VMEM(side, f32)],
+        flops=cost,
+        name="far_far",
+    )
+    back_pair = swapped(far_grad_pair, key_mate)
+    far_grad_query, grad_key, grad_value = call(
+        far_near_kernel,
+        (halves, far_query_side, key_side, first_far_query, own[1], own[2]),
+        [SMEM] + [VMEM] * 5,
+        [(side, bf16), (side, f32), (side, f32)],
+        [row_scratch(), row_scratch(), pltpu.VMEM(side, f32)],
+        flops=cost,
+        name="far_near",
     )
     back_query = swapped(far_grad_query, query_mate)
-    back_pair = swapped(far_grad_pair, key_mate)
     (joined,) = call(
         join_kernel,
         (grad_query, grad_key, grad_value, back_query, back_pair),
@@ -289,7 +356,9 @@
             (returned,),
             [VMEM],
             [((ROWS, OWNERS * HEAD_DIM), bf16)] * 3,
+            [pltpu.SemaphoreType.DMA((3, OWNERS))],
             name="unpack",
+            space=HBM,
         )
     )
 

time: 118 us -> 111 us (0.941)
  local copies, waits for them, and re-layouts: 6.07 us -> 1.33 us
  waiting for transfers between devices: 13.5 us -> 8.84 us
  Pallas kernels: 12.8 us -> 16.2 us
    unnamed x12 -> x2, local copies, waits for them, and re-layouts: 4.75 us -> 0.01 us
    ppermute x4, waiting for transfers between devices: 13.5 us -> 8.84 us  [swapped(): return lax.ppermute(value, 'blk', pairs)]
    pallas_call x6 -> x8, Pallas kernels: 12.8 us -> 16.2 us  [call(): pl.pallas_call(kernel, out_shape=[jax.ShapeDtypeStruct(shape, dtype) for...]
  transfers between devices with their start and end apart: 4 -> 4, of which waited for: 3 -> 3; matrix products, arithmetic and copies ran while one was open for 1% -> 1% of each run, Pallas kernels for 3% -> 9%
where the time goes in v2:
time: 111 us; the launch traced here: 110 us
  blocking collectives  66.6 us (60%)
  Pallas kernels  16.2 us (15%)
  starting transfers between devices  12.7 us (11%)
  waiting for transfers between devices  8.84 us (8%)
  between operations  4.64 us (4%)
  local copies, waits for them, and re-layouts  1.33 us (1%)
    all_to_all x1, blocking collectives, per_device(): lax.all_to_all(packed, 'ulysses', split_axis=0, concat_axis=0, tiled=True)  40.4 us
    all_to_all x1, blocking collectives, per_device(): lax.all_to_all(joined, 'ulysses', split_axis=0, concat_axis=0, tiled=True)  26.2 us
    pallas_call x8, Pallas kernels, call(): pl.pallas_call(kernel, out_shape=[jax.ShapeDtypeStruct(shape, dtype) for...  16.2 us
    ppermute x4, starting transfers between devices, swapped(): return lax.ppermute(value, 'blk', pairs)  12.7 us
    ppermute x4, waiting for transfers between devices, swapped(): return lax.ppermute(value, 'blk', pairs)  8.84 us
  transfers between devices with their start and end apart: 4, of which 3 were waited for; matrix products, arithmetic and copies ran while one was open for 1% of the time, Pallas kernels for 9%

profile of v2, /device:TPU:56, one launch (start us, length us, event | category | flops | bytes accessed | tf_op | source)
XLA Modules:
  0.0 110.4 jit_solution(12021322269258854622)
XLA Ops:
  0.6 2.3 %pack.1 = bf16[8,528,128]{2,1,0:T(8,128)(2,1)S(1)} custom-call(bf16[128,1024]{1,0:T(8,128)(2,1)} %query_ref.1, bf16[128,1024]{1,0:T(8,128)(2,1)} %key_ref.1, bf16[128,1024]{1,0:T(8,128)(2,1)} %value_ref.1, bf16[128,1024]{1,0:T(8,128)(2,1)} %output_ref.1, bf16[128,1024]{1,0:T(8,128)(2,1)} %cotangent_ref.1), custom_call_target="tpu_custom_call" | custom-call | bytes 4194304 | tf_op jit(solution)/shard_map/pack/pallas_call | solution.py:247
  2.9 0.0 copy-start
  2.9 40.4 %all_to_all.10.moved_ref = bf16[8,528,128]{2,1,0:T(8,128)(2,1)S(1)} all-to-all(bf16[8,528,128]{2,1,0:T(8,128)(2,1)S(1)} %pack.1), channel_id=1, replica_groups=mesh['ulysses'=8,'blk'=64] {'ulysses'}, dimensions={0} | all-to-all | bytes 2162688 | tf_op jit(solution)/shard_map/all_to_all | solution.py:296
  43.3 0.0 copy-done
  43.3 0.1 split.1
  43.4 4.7 %collective-permute-start = (bf16[8,256,128]{2,1,0:T(8,128)(2,1)S(1)}, bf16[8,256,128]{2,1,0:T(8,128)(2,1)S(1)}, u32[]{:S(2)}, u32[]{:S(2)}) collective-permute-start(bf16[8,256,128]{2,1,0:T(8,128)(2,1)S(1)} %get-tuple-element.17.key_side_ref), channel_id=1, source_target_pairs={{0,48},{1,49},{2,50},{3,51},{4,52},{5,53},{6,54},{7,55},{8,56},{9,... | collective-permute-start | bytes 1572872 | tf_op jit(solution)/shard_map/ppermute | solution.py:274
  48.1 2.1 %collective-permute-start.1 = (bf16[8,272,128]{2,1,0:T(8,128)(2,1)S(1)}, bf16[8,272,128]{2,1,0:T(8,128)(2,1)S(1)}, u32[]{:S(2)}, u32[]{:S(2)}) collective-permute-start(bf16[8,272,128]{2,1,0:T(8,128)(2,1)S(1)} %get-tuple-element.16.query_side_ref), channel_id=1, source_target_pairs={{0,16},{1,17},{2,18},{3,19},{4,20},{5,21},{6,22},{7,23},{8,24},{9,... | collective-permute-start | bytes 1671176 | tf_op jit(solution)/shard_map/ppermute | solution.py:274
  50.3 1.3 %fusion = (s32[1]{0:T(128)}, s32[1]{0:T(128)}, s32[1]{0:T(128)}) fusion(s32[65536]{0:T(1024)} %param.13, s32[]{:T(128)S(6)} %select_n.23, s32[]{:T(128)S(6)} %select_n.22, s32[]{:T(128)S(6)} %select_n.24), kind=kLoop, calls=%fused_computation.1 | loop fusion | bytes 36 | tf_op jit(solution)/shard_map/dynamic_slice | solution.py:278
  55.5 0.1 add_convert_fusion.halves_ref
  55.6 3.2 %own.1 = (f32[8,128,128]{2,1,0:T(8,128)S(1)}, f32[8,128,128]{2,1,0:T(8,128)S(1)}, f32[8,128,128]{2,1,0:T(8,128)S(1)}) custom-call(bf16[8,272,128]{2,1,0:T(8,128)(2,1)S(1)} %get-tuple-element.16.query_side_ref, bf16[8,256,128]{2,1,0:T(8,128)(2,1)S(1)} %get-tuple-element.17.key_side_ref), custom_call_target="tpu_custom_call" | custom-call | flops 838860800 | bytes 4194304 | tf_op jit(solution)/shard_map/own/pallas_call | solution.py:247
  58.8 1.4 %collective-permute-done.far_key_side_ref = bf16[8,256,128]{2,1,0:T(8,128)(2,1)S(1)} collective-permute-done((bf16[8,256,128]{2,1,0:T(8,128)(2,1)S(1)}, bf16[8,256,128]{2,1,0:T(8,128)(2,1)S(1)}, u32[]{:S(2)}, u32[]{:S(2)}) %collective-permute-start) | collective-permute-done | bytes 524320 | tf_op jit(solution)/shard_map/ppermute | solution.py:274
  60.1 3.2 %near_far.1 = (f32[8,128,128]{2,1,0:T(8,128)S(1)}, f32[8,128,128]{2,1,0:T(8,128)S(1)}, f32[8,128,128]{2,1,0:T(8,128)S(1)}) custom-call(s32[3]{0:T(128)S(1)} %add_convert_fusion.halves_ref, bf16[8,272,128]{2,1,0:T(8,128)(2,1)S(1)} %get-tuple-element.16.query_side_ref, bf16[8,256,128]{2,1,0:T(8,128)(2,1)S(1)} %collective-permute-done.far_key_side_ref, ...), custom_call_target="tpu_custom_call" | custom-call | flops 671088640 | bytes 4194304 | tf_op jit(solution)/shard_map/near_far/pallas_call | solution.py:247
  63.3 0.7 collective-permute-done.1.far_query_side_ref
  64.0 3.1 %far_far.1 = (f32[8,128,128]{2,1,0:T(8,128)S(1)}, bf16[2,8,128,128]{3,2,1,0:T(8,128)(2,1)S(1)}) custom-call(s32[3]{0:T(128)S(1)} %add_convert_fusion.halves_ref, bf16[8,272,128]{2,1,0:T(8,128)(2,1)S(1)} %collective-permute-done.1.far_query_side_ref, bf16[8,256,128]{2,1,0:T(8,128)(2,1)S(1)} %collective-permute-done.far_key_side_ref, ...), custom_call_target="tpu_custom_call" | custom-call | flops 671088640 | bytes 4194304 | tf_op jit(solution)/shard_map/far_far/pallas_call | solution.py:247
  67.1 4.0 %collective-permute-start.3 = (bf16[2,8,128,128]{3,2,1,0:T(8,128)(2,1)S(1)}, bf16[2,8,128,128]{3,2,1,0:T(8,128)(2,1)S(1)}, u32[]{:S(2)}, u32[]{:S(2)}) collective-permute-start(bf16[2,8,128,128]{3,2,1,0:T(8,128)(2,1)S(1)} %get-tuple-element.28), channel_id=1, source_target_pairs={{0,48},{1,49},{2,50},{3,51},{4,52},{5,53},{6,54},{7,55},{8,56},{9,... | collective-permute-start | bytes 1572872 | tf_op jit(solution)/shard_map/ppermute | solution.py:274
  71.1 3.2 %far_near.1 = (bf16[8,128,128]{2,1,0:T(8,128)(2,1)S(1)}, f32[8,128,128]{2,1,0:T(8,128)S(1)}, f32[8,128,128]{2,1,0:T(8,128)S(1)}) custom-call(s32[3]{0:T(128)S(1)} %add_convert_fusion.halves_ref, bf16[8,272,128]{2,1,0:T(8,128)(2,1)S(1)} %collective-permute-done.1.far_query_side_ref, bf16[8,256,128]{2,1,0:T(8,128)(2,1)S(1)} %get-tuple-element.17.key_side_ref, ...), custom_call_target="tpu_custom_call" | custom-call | flops 671088640 | bytes 4194304 | tf_op jit(solution)/shard_map/far_near/pallas_call | solution.py:247
  74.3 1.9 %collective-permute-start.2 = (bf16[8,128,128]{2,1,0:T(8,128)(2,1)S(1)}, bf16[8,128,128]{2,1,0:T(8,128)(2,1)S(1)}, u32[]{:S(2)}, u32[]{:S(2)}) collective-permute-start(bf16[8,128,128]{2,1,0:T(8,128)(2,1)S(1)} %get-tuple-element.27), channel_id=1, source_target_pairs={{0,16},{1,17},{2,18},{3,19},{4,20},{5,21},{6,22},{7,23},{8,24},{9,... | collective-permute-start | bytes 786440 | tf_op jit(solution)/shard_map/ppermute | solution.py:274
  76.2 6.8 %collective-permute-done.2.back_query_ref = bf16[8,128,128]{2,1,0:T(8,128)(2,1)S(1)} collective-permute-done((bf16[8,128,128]{2,1,0:T(8,128)(2,1)S(1)}, bf16[8,128,128]{2,1,0:T(8,128)(2,1)S(1)}, u32[]{:S(2)}, u32[]{:S(2)}) %collective-permute-start.2) | collective-permute-done | bytes 262176 | tf_op jit(solution)/shard_map/ppermute | solution.py:274
  83.0 0.0 collective-permute-done.3.back_pair_ref
  83.0 0.1 join.1
  83.2 26.2 %all_to_all.11.moved_ref = bf16[8,384,128]{2,1,0:T(8,128)(2,1)S(1)} all-to-all(bf16[8,384,128]{2,1,0:T(8,128)(2,1)S(1)} %join.1), channel_id=1, replica_groups=mesh['ulysses'=8,'blk'=64] {'ulysses'}, dimensions={0} | all-to-all | bytes 1572864 | tf_op jit(solution)/shard_map/all_to_all | solution.py:352
  109.3 1.1 unpack.1
Async XLA Ops:
  2.9 40.5 %copy-start = (f32[1024,1]{0,1:T(1,128)S(1)}, f32[1024,1]{0,1:T(1,128)}, u32[]{:S(2)}) copy-start(f32[1024,1]{0,1:T(1,128)} %param.12) | copy-start | bytes 12292
  43.4 16.7 %collective-permute-start = (bf16[8,256,128]{2,1,0:T(8,128)(2,1)S(1)}, bf16[8,256,128]{2,1,0:T(8,128)(2,1)S(1)}, u32[]{:S(2)}, u32[]{:S(2)}) collective-permute-start(bf16[8,256,128]{2,1,0:T(8,128)(2,1)S(1)} %get-tuple-element.17.key_side_ref), channel_id=1, source_target_pairs={{0,48},{1,49},{2,50},{3,51},{4,52},{5,53},{6,54},{7,55},{8,56},{9,... | collective-permute-start | bytes 1572872 | tf_op jit(solution)/shard_map/ppermute | solution.py:274
  48.1 15.9 %collective-permute-start.1 = (bf16[8,272,128]{2,1,0:T(8,128)(2,1)S(1)}, bf16[8,272,128]{2,1,0:T(8,128)(2,1)S(1)}, u32[]{:S(2)}, u32[]{:S(2)}) collective-permute-start(bf16[8,272,128]{2,1,0:T(8,128)(2,1)S(1)} %get-tuple-element.16.query_side_ref), channel_id=1, source_target_pairs={{0,16},{1,17},{2,18},{3,19},{4,20},{5,21},{6,22},{7,23},{8,24},{9,... | collective-permute-start | bytes 1671176 | tf_op jit(solution)/shard_map/ppermute | solution.py:274
  67.1 15.9 %collective-permute-start.3 = (bf16[2,8,128,128]{3,2,1,0:T(8,128)(2,1)S(1)}, bf16[2,8,128,128]{3,2,1,0:T(8,128)(2,1)S(1)}, u32[]{:S(2)}, u32[]{:S(2)}) collective-permute-start(bf16[2,8,128,128]{3,2,1,0:T(8,128)(2,1)S(1)} %get-tuple-element.28), channel_id=1, source_target_pairs={{0,48},{1,49},{2,50},{3,51},{4,52},{5,53},{6,54},{7,55},{8,56},{9,... | collective-permute-start | bytes 1572872 | tf_op jit(solution)/shard_map/ppermute | solution.py:274
  74.3 8.7 %collective-permute-start.2 = (bf16[8,128,128]{2,1,0:T(8,128)(2,1)S(1)}, bf16[8,128,128]{2,1,0:T(8,128)(2,1)S(1)}, u32[]{:S(2)}, u32[]{:S(2)}) collective-permute-start(bf16[8,128,128]{2,1,0:T(8,128)(2,1)S(1)} %get-tuple-element.27), channel_id=1, source_target_pairs={{0,16},{1,17},{2,18},{3,19},{4,20},{5,21},{6,22},{7,23},{8,24},{9,... | collective-permute-start | bytes 786440 | tf_op jit(solution)/shard_map/ppermute | solution.py:274

commit v3 on v0

--- a/solution.py
+++ b/solution.py
@@ -1,9 +1,488 @@
 import jax
 import jax.numpy as jnp
 from jax import lax
+from jax.experimental import pallas as pl
+from jax.experimental.pallas import tpu as pltpu
 from jax.sharding import PartitionSpec as P
 
 SPAN = 4
+HEAD_DIM = 128
+LOG2E = 1.4426950408889634
+SCALE = HEAD_DIM ** -0.5
+ROWS = 128
+HEADS = 8
+OWNERS = 8
+HALF = 4
+CHUNK = 256
+EXTRA = 16
+PART = 4 * ROWS + EXTRA
+AXES = ("ulysses", "blk")
+f32 = jnp.float32
+bf16 = jnp.bfloat16
+VMEM = pl.BlockSpec(memory_space=pltpu.VMEM)
+SMEM = pl.BlockSpec(memory_space=pltpu.SMEM)
+HBM = pl.BlockSpec(memory_space=pltpu.HBM)
+PARAMS = pltpu.CompilerParams(vmem_limit_bytes=24 * 1024 * 1024)
+
+
+def three_terms(row):
+    high = row.astype(bf16).astype(f32)
+    rest = row - high
+    middle = rest.astype(bf16).astype(f32)
+    return (high, middle, rest - middle)
+
+
+def chunk_at(level, pair):
+    return jnp.where(
+        level == 0,
+        2 * pair,
+        jnp.where(level == 1, 2 * pair + 1, jnp.where(level == 2, 14 - 2 * pair, 15 - 2 * pair)),
+    )
+
+
+def rank_at(level, pair):
+    return jnp.where(level < 2, pair, 3 - pair)
+
+
+def fill_table(table_ref, pairs, role, place, level):
+    def pick(at):
+        value = pairs[0]
+        for index in range(1, SPAN):
+            value = jnp.where(at == index, pairs[index], value)
+        return value
+
+    sides = ((place, level), (SPAN - 1 - place, level ^ 1), (place ^ 1, 3 - level))
+    for side, (run, height) in enumerate(sides):
+        pair = pick(run)
+        for index in range(4):
+            over_x = chunk_at(jnp.int32(index), pair)
+            over_z = 2 * index + jnp.where(height < 2, height, height + 6)
+            table_ref[4 * side + index] = jnp.where(role == 0, over_x, over_z)
+    for slot in range(SPAN):
+        table_ref[12 + slot] = jnp.where(role == 0, slot, rank_at(level, pairs[slot]))
+        table_ref[16 + slot] = pairs[slot]
+
+
+def pack_kernel(
+    where_ref,
+    query_ref,
+    key_ref,
+    value_ref,
+    output_ref,
+    cotangent_ref,
+    positions_ref,
+    packed_ref,
+    table_ref,
+    output_here,
+    places,
+    arrived,
+    places_arrived,
+):
+    role, place, level, line, stride = (where_ref[index] for index in range(5))
+    run_rows = OWNERS * ROWS
+    first_places = []
+    for run in range(SPAN):
+        start = pl.multiple_of((run * stride + line) * run_rows, run_rows)
+        first_places.append(
+            pltpu.make_async_copy(
+                positions_ref.at[pl.ds(start, 128)], places.at[run], places_arrived.at[run]
+            )
+        )
+
+    def copies(index, source):
+        for head in range(HEADS):
+            columns = pl.ds(head * HEAD_DIM, HEAD_DIM)
+            target = output_here.at[head]
+            if index < 4:
+                target = packed_ref.at[head % 2, head // 2, pl.ds(index * ROWS, ROWS), :]
+            yield pltpu.make_async_copy(source.at[:, columns], target, arrived.at[index, head])
+
+    sources = (query_ref, cotangent_ref, key_ref, value_ref, output_ref)
+    moves = [list(copies(index, source)) for index, source in enumerate(sources)]
+    for index in (1, 4, 0, 2, 3):
+        for move in moves[index]:
+            move.start()
+    for move in first_places:
+        move.start()
+    row = lax.broadcasted_iota(jnp.int32, (EXTRA, ROWS), 0)
+    for head in range(HEADS):
+        moves[1][head].wait()
+        moves[4][head].wait()
+        cotangent = packed_ref[head % 2, head // 2, 128:256, :].astype(f32)
+        delta = jnp.sum((cotangent * output_here[head].astype(f32)).T, axis=0, keepdims=True)
+        high, middle, low = three_terms(delta)
+        rows = jnp.where(row == 0, high, jnp.where(row == 1, middle, jnp.where(row == 2, low, 0.0)))
+        packed_ref[head % 2, head // 2, 512:528, :] = rows.astype(bf16)
+    for move in first_places:
+        move.wait()
+    pairs = [
+        jnp.minimum(lax.div(places[run, 0], jnp.int32(2 * CHUNK)), SPAN - 1) for run in range(SPAN)
+    ]
+    fill_table(table_ref, pairs, role, place, level)
+    for index in (0, 2, 3):
+        for move in moves[index]:
+            move.wait()
+
+
+def with_lse(rows, lse):
+    row = lax.broadcasted_iota(jnp.int32, (EXTRA, ROWS), 0)
+    rows = rows.astype(f32)
+    for group in range(lse.shape[0]):
+        for index, term in enumerate(three_terms(lse[group : group + 1, :])):
+            rows = jnp.where(row == 3 + 3 * group + index, term, rows)
+    return rows.astype(bf16)
+
+
+def arrange_kernel(moved_ref, lse_ref, slots_ref):
+    for owner in range(2):
+        lse = lse_ref[HALF * owner : HALF * (owner + 1), :]
+        for slot in range(SPAN):
+            slots_ref[slot, owner, 0:512, :] = moved_ref[owner, slot, 0:512, :]
+            slots_ref[slot, owner, 512:528, :] = with_lse(moved_ref[owner, slot, 512:528, :], lse)
+
+
+def split_kernel(
+    where_ref,
+    table_ref,
+    slots_ref,
+    lse_ref,
+    query_side_ref,
+    key_side_ref,
+    first_ref,
+    second_ref,
+    run_lse_ref,
+):
+    role, level = where_ref[0], where_ref[2]
+    for slot in range(SPAN):
+        for owner in range(2):
+            block = 2 * table_ref[12 + slot] + owner
+            query_side_ref[block, 0:256, :] = slots_ref[slot, owner, 0:256, :]
+            key_side_ref[block, 0:256, :] = slots_ref[slot, owner, 256:512, :]
+            rows = slots_ref[slot, owner, 512:528, :]
+            at = 2 * slot + owner
+            query_side_ref[block, 256:272, :] = with_lse(rows, lse_ref[at : at + 1, :])
+            key_side_ref[block, 256:272, :] = jnp.zeros_like(rows)
+            rows = rows.astype(f32)
+            for group in range(HALF):
+                first = 3 + 3 * group
+                total = rows[first : first + 1] + rows[first + 1 : first + 2]
+                run_lse_ref[slot, pl.ds(HALF * owner + group, 1), :] = (
+                    total + rows[first + 2 : first + 3]
+                )
+
+    @pl.when(role == 0)
+    def _():
+        first_ref[...] = key_side_ref[...]
+
+    @pl.when(role != 0)
+    def _():
+        first_ref[...] = query_side_ref[...]
+
+    @pl.when((role == 0) | (level > 1))
+    def _():
+        second_ref[...] = query_side_ref[...]
+
+    @pl.when((role != 0) & (level < 2))
+    def _():
+        second_ref[...] = key_side_ref[...]
+
+
+def lse_kernel(where_ref, table_ref, run_lse_ref, *rest):
+    shifted_refs, given_ref = rest[:-1], rest[-1]
+    place, level = where_ref[1], where_ref[2]
+    shift = lax.rem(level - place + SPAN, SPAN)
+
+    def fill(source_ref):
+        for index, height in enumerate((level, level ^ 1, 3 - level)):
+            for run in range(SPAN):
+                rank = rank_at(height, table_ref[16 + run])
+                rows = source_ref[run, pl.ds(2 * height, 2), :]
+                given_ref[index, pl.ds(2 * rank, 2), :] = rows
+
+    for index, source_ref in enumerate((run_lse_ref, *shifted_refs)):
+
+        @pl.when(shift == index)
+        def _():
+            fill(source_ref)
+
+
+def read_rows(query_side_ref, lse_ref, delta_ref, given=None):
+    for block in range(OWNERS):
+        rows = query_side_ref[block, 256:272, :].astype(f32)
+        half, part = block // HALF, block % HALF
+        columns = slice(part * ROWS, (part + 1) * ROWS)
+        delta_ref[half, :, columns] = rows[0:1] + rows[1:2] + rows[2:3]
+        lse = rows[3:4] + rows[4:5] + rows[5:6]
+        if given is not None:
+            given_ref, index = given
+            lse = given_ref[index, block : block + 1, :]
+        lse_ref[half, :, columns] = lse * LOG2E
+
+
+def nt(left, right):
+    return lax.dot_general(left, right, (((1,), (1,)), ((), ())), preferred_element_type=f32)
+
+
+def nn(left, right):
+    return lax.dot_general(left, right, (((1,), (0,)), ((), ())), preferred_element_type=f32)
+
+
+def tn(left, right):
+    return lax.dot_general(left, right, (((0,), (0,)), ((), ())), preferred_element_type=f32)
+
+
+def block_grads(query_half, key_half, query_refs, key_refs, chunks):
+    query_side_ref, lse_ref, delta_ref, grad_query_ref = query_refs
+    key_side_ref, grad_key_ref, grad_value_ref = key_refs
+    size = HALF * ROWS
+    keys_at = pl.ds(key_half * HALF, HALF)
+    queries_at = pl.ds(query_half * HALF, HALF)
+    key = key_side_ref[keys_at, 0:128, :].reshape(size, HEAD_DIM)
+    value = key_side_ref[keys_at, 128:256, :].reshape(size, HEAD_DIM)
+    query = query_side_ref[queries_at, 0:128, :].reshape(size, HEAD_DIM)
+    cotangent = query_side_ref[queries_at, 128:256, :].reshape(size, HEAD_DIM)
+    scores = nt(key, query)
+    probs = jnp.exp2(scores * (SCALE * LOG2E) - lse_ref[query_half])
+    if chunks is not None:
+        (query_low, query_high), (key_low, key_high) = chunks
+        at_query = lax.broadcasted_iota(jnp.int32, (1, size), 1)
+        at_key = lax.broadcasted_iota(jnp.int32, (size, 1), 0)
+        at_query += jnp.where(at_query < CHUNK, query_low * CHUNK, query_high * CHUNK - CHUNK)
+        at_key += jnp.where(at_key < CHUNK, key_low * CHUNK, key_high * CHUNK - CHUNK)
+        probs = jnp.where(at_query >= at_key, probs, 0.0)
+    grad_probs = nt(value, cotangent)
+    grad_scores = (probs * (grad_probs - delta_ref[query_half])).astype(bf16)
+    shape = (HALF, ROWS, HEAD_DIM)
+    grad_value_ref[keys_at] += nn(probs.astype(bf16), cotangent).reshape(shape)
+    grad_key_ref[keys_at] += nn(grad_scores, query).reshape(shape)
+    grad_query_ref[queries_at] += tn(grad_scores, key).reshape(shape)
+
+
+def stairs_grads(table_ref, query_side, key_side, query_refs, key_refs):
+    def chunks(half):
+        at_query, at_key = 4 * query_side + 2 * half, 4 * key_side + 2 * half
+        return (
+            (table_ref[at_query], table_ref[at_query + 1]),
+            (table_ref[at_key], table_ref[at_key + 1]),
+        )
+
+    block_grads(1, 0, query_refs, key_refs, None)
+    block_grads(0, 0, query_refs, key_refs, chunks(0))
+    block_grads(1, 1, query_refs, key_refs, chunks(1))
+
+
+def paired_grads(table_ref, query_side, key_side, query_refs, key_refs):
+    half = jnp.where(table_ref[4 * query_side] < table_ref[4 * key_side], 1, 0)
+    block_grads(1, 0, query_refs, key_refs, None)
+    block_grads(half, half, query_refs, key_refs, None)
+
+
+def whole_grads(query_refs, key_refs):
+    for query_half in range(2):
+        for key_half in range(2):
+            block_grads(query_half, key_half, query_refs, key_refs, None)
+
+
+def own_kernel(
+    where_ref,
+    table_ref,
+    query_side_ref,
+    key_side_ref,
+    given_ref,
+    last_query_ref,
+    last_key_ref,
+    last_value_ref,
+    grad_query_ref,
+    grad_key_ref,
+    grad_value_ref,
+    *rows,
+):
+    grad_query_ref[...] = last_query_ref[...]
+    grad_key_ref[...] = last_key_ref[...]
+    grad_value_ref[...] = last_value_ref[...]
+
+    @pl.when(where_ref[0] == 0)
+    def _():
+        read_rows(query_side_ref, *rows)
+
+    @pl.when(where_ref[0] != 0)
+    def _():
+        read_rows(query_side_ref, *rows, (given_ref, 0))
+
+    query_refs = (query_side_ref, *rows, grad_query_ref)
+    stairs_grads(table_ref, 0, 0, query_refs, (key_side_ref, grad_key_ref, grad_value_ref))
+
+
+def first_kernel(
+    where_ref,
+    table_ref,
+    query_side_ref,
+    key_side_ref,
+    first_ref,
+    given_ref,
+    grad_query_ref,
+    grad_key_ref,
+    grad_value_ref,
+    first_sum_ref,
+    first_value_ref,
+    *rows,
+):
+    for ref in (grad_query_ref, grad_key_ref, grad_value_ref, first_sum_ref, first_value_ref):
+        ref[...] = jnp.zeros_like(ref)
+
+    @pl.when(where_ref[0] == 0)
+    def _():
+        read_rows(query_side_ref, *rows)
+        query_refs = (query_side_ref, *rows, grad_query_ref)
+        paired_grads(table_ref, 0, 1, query_refs, (first_ref, first_sum_ref, first_value_ref))
+
+    @pl.when(where_ref[0] != 0)
+    def _():
+        read_rows(first_ref, *rows, (given_ref, 1))
+        query_refs = (first_ref, *rows, first_sum_ref)
+        stairs_grads(table_ref, 1, 0, query_refs, (key_side_ref, grad_key_ref, grad_value_ref))
+
+
+def second_kernel(
+    where_ref,
+    table_ref,
+    key_side_ref,
+    first_ref,
+    second_ref,
+    given_ref,
+    last_key_ref,
+    last_value_ref,
+    last_sum_ref,
+    last_far_value_ref,
+    grad_key_ref,
+    grad_value_ref,
+    query_sum_ref,
+    late_back_ref,
+    key_back_ref,
+    key_sum,
+    value_sum,
+    *rows,
+):
+    role, level = where_ref[0], where_ref[2]
+    grad_key_ref[...] = last_key_ref[...]
+    grad_value_ref[...] = last_value_ref[...]
+
+    @pl.when(role == 0)
+    def _():
+        key_sum[...] = last_sum_ref[...]
+        value_sum[...] = last_far_value_ref[...]
+        query_sum_ref[...] = jnp.zeros_like(query_sum_ref)
+        read_rows(second_ref, *rows)
+        query_refs = (second_ref, *rows, query_sum_ref)
+        paired_grads(table_ref, 2, 1, query_refs, (first_ref, key_sum, value_sum))
+
+    @pl.when(role != 0)
+    def _():
+        query_sum_ref[...] = last_sum_ref[...]
+        key_sum[...] = jnp.zeros_like(key_sum)
+        value_sum[...] = jnp.zeros_like(value_sum)
+
+    @pl.when((role != 0) & (level < 2))
+    def _():
+        read_rows(second_ref, *rows, (given_ref, 2))
+        query_refs = (second_ref, *rows, key_sum)
+        whole_grads(query_refs, (key_side_ref, grad_key_ref, grad_value_ref))
+        late_back_ref[...] = (key_sum[...] * SCALE).astype(bf16)
+
+    @pl.when((role != 0) & (level > 1))
+    def _():
+        read_rows(first_ref, *rows, (given_ref, 1))
+        query_refs = (first_ref, *rows, query_sum_ref)
+        whole_grads(query_refs, (second_ref, key_sum, value_sum))
+
+    @pl.when((role == 0) | (level > 1))
+    def _():
+        key_back_ref[0] = (key_sum[...] * SCALE).astype(bf16)
+        key_back_ref[1] = value_sum[...].astype(bf16)
+
+
+def third_kernel(
+    where_ref,
+    table_ref,
+    key_side_ref,
+    second_ref,
+    last_key_ref,
+    last_value_ref,
+    last_sum_ref,
+    grad_key_ref,
+    grad_value_ref,
+    query_back_ref,
+    query_sum,
+    *rows,
+):
+    grad_key_ref[...] = last_key_ref[...]
+    grad_value_ref[...] = last_value_ref[...]
+    query_sum[...] = last_sum_ref[...]
+
+    @pl.when(where_ref[0] == 0)
+    def _():
+        read_rows(second_ref, *rows)
+        query_refs = (second_ref, *rows, query_sum)
+        paired_grads(table_ref, 2, 0, query_refs, (key_side_ref, grad_key_ref, grad_value_ref))
+
+    query_back_ref[...] = (query_sum[...] * SCALE).astype(bf16)
+
+
+def join_kernel(
+    table_ref,
+    grad_query_ref,
+    grad_key_ref,
+    grad_value_ref,
+    query_back_ref,
+    late_back_ref,
+    key_back_ref,
+    slots_ref,
+):
+    for slot in range(SPAN):
+        for owner in range(2):
+            at = 2 * table_ref[12 + slot] + owner
+            back = query_back_ref[at].astype(f32) + late_back_ref[at].astype(f32)
+            sums = (
+                grad_query_ref[at] * SCALE + back,
+                grad_key_ref[at] * SCALE + key_back_ref[0, at].astype(f32),
+                grad_value_ref[at] + key_back_ref[1, at].astype(f32),
+            )
+            for index, total in enumerate(sums):
+                slots_ref[slot, owner, index * ROWS : (index + 1) * ROWS, :] = total.astype(bf16)
+
+
+def turn_kernel(slots_ref, owners_ref):
+    for owner in range(2):
+        for slot in range(SPAN):
+            owners_ref[owner, slot] = slots_ref[slot, owner]
+
+
+def unpack_kernel(moved_ref, grad_query_ref, grad_key_ref, grad_value_ref, sent):
+    moves = []
+    for head in range(HEADS):
+        columns = pl.ds(head * HEAD_DIM, HEAD_DIM)
+        for index, target in enumerate((grad_query_ref, grad_key_ref, grad_value_ref)):
+            source = moved_ref.at[head % 2, head // 2, pl.ds(index * ROWS, ROWS), :]
+            moves.append(
+                pltpu.make_async_copy(source, target.at[:, columns], sent.at[index, head])
+            )
+    for move in moves:
+        move.start()
+    for move in moves:
+        move.wait()
+
+
+def call(kernel, args, specs, outs, scratch=(), flops=0, moved=4 << 20, name=None, spaces=None):
+    return pl.pallas_call(
+        kernel,
+        out_shape=[jax.ShapeDtypeStruct(shape, dtype) for shape, dtype in outs],
+        in_specs=specs,
+        out_specs=[VMEM] * len(outs) if spaces is None else spaces,
+        scratch_shapes=list(scratch),
+        compiler_params=PARAMS,
+        cost_estimate=pl.CostEstimate(flops=flops, bytes_accessed=moved, transcendentals=0),
+        name=name,
+    )(*args)
 
 
 def passed_along(value, axis, steps):
@@ -86,7 +565,7 @@
     )
 
 
-def per_device(queries, key_rows, value_rows, attn_output, grad_output, logsumexp, positions):
+def any_order(queries, key_rows, value_rows, attn_output, grad_output, logsumexp, positions):
     heads_dev = logsumexp.shape[1]
     moved = (
         lax.all_to_all(queries, "ulysses", split_axis=1, concat_axis=0, tiled=True),
@@ -148,24 +627,188 @@
     return (back[0], back[1], back[2])
 
 
+def row_scratch():
+    return pltpu.VMEM((2, 1, HALF * ROWS), f32)
+
+
+def per_device(queries, key_rows, value_rows, attn_output, grad_output, logsumexp, positions):
+    blk_count = lax.axis_size("blk")
+    stride = blk_count // SPAN
+    rank, here = lax.axis_index("ulysses"), lax.axis_index("blk")
+    line = here % stride
+    role = (rank % 2) ^ (2 * line // stride)
+    where = jnp.stack([role, here // stride, rank // 2, line, jnp.int32(stride)])
+
+    def index_of(role, place, level, at):
+        core = role ^ (2 * at // stride)
+        return (2 * level + core) * blk_count + place * stride + at
+
+    spots = [(p, z, at) for p in range(SPAN) for z in range(SPAN) for at in range(stride)]
+
+    def swapped(value, over_x, over_z, levels=range(SPAN)):
+        pairs = []
+        for p, z, at in spots:
+            if over_x is not None:
+                pairs.append((index_of(0, p, z, at), index_of(0, over_x(p), z, at)))
+            if z in levels:
+                pairs.append((index_of(1, p, z, at), index_of(1, p, over_z(z), at)))
+        return lax.ppermute(value, AXES, pairs)
+
+    mate = lambda at: at ^ 1
+    mirror = lambda at: SPAN - 1 - at
+
+    def level_shift(value, shift):
+        pairs = [
+            (index_of(1, p, p, at), index_of(1, p, (p + shift) % SPAN, at))
+            for p in range(SPAN)
+            for at in range(stride)
+        ]
+        return lax.ppermute(value, AXES, pairs)
+
+    core_groups = [sorted(index_of(role, p, z, at) for role in range(2)) for p, z, at in spots]
+    over_z = lambda role: [
+        [index_of(role, p, z, at) for z in range(SPAN)] for p in range(SPAN) for at in range(stride)
+    ]
+    over_x = lambda role: [
+        [index_of(role, p, z, at) for p in range(SPAN)] for z in range(SPAN) for at in range(stride)
+    ]
+    head_groups = over_z(0) + over_x(1)
+
+    def exchanged(value, groups):
+        return lax.all_to_all(
+            value, AXES, split_axis=0, concat_axis=0, axis_index_groups=groups, tiled=True
+        )
+
+    side = (OWNERS, ROWS, HEAD_DIM)
+    lse = logsumexp.reshape(OWNERS, ROWS)
+    tokens = [
+        pltpu.with_memory_space_constraint(value, pltpu.HBM)
+        for value in (queries, key_rows, value_rows, attn_output, grad_output, positions)
+    ]
+    packed, table = call(
+        pack_kernel,
+        (where, *tokens),
+        [SMEM] + [HBM] * 6,
+        [((2, SPAN, PART, HEAD_DIM), bf16), ((20,), jnp.int32)],
+        [
+            pltpu.VMEM((HEADS, ROWS, HEAD_DIM), bf16),
+            pltpu.SMEM((SPAN, 128), jnp.int32),
+            pltpu.SemaphoreType.DMA((5, HEADS)),
+            pltpu.SemaphoreType.DMA((SPAN,)),
+        ],
+        name="pack",
+        spaces=[VMEM, SMEM],
+    )
+    (slots,) = call(
+        arrange_kernel,
+        (exchanged(packed, core_groups), lse),
+        [VMEM] * 2,
+        [((SPAN, 2, PART, HEAD_DIM), bf16)],
+        name="arrange",
+    )
+    card = ((OWNERS, 272, HEAD_DIM), bf16)
+    rows = [row_scratch(), row_scratch()]
+    query_side, key_side, first_out, second_out, run_lse = call(
+        split_kernel,
+        (where, table, exchanged(slots, head_groups), lse),
+        [SMEM] * 2 + [VMEM] * 2,
+        [card] * 4 + [((SPAN, OWNERS, ROWS), f32)],
+        name="split",
+    )
+    first = swapped(first_out, mirror, mate)
+    second = swapped(second_out, mate, mirror)
+    cost = 10 * 128 * 2 * 512 * 512
+    (given,) = call(
+        lse_kernel,
+        (where, table, run_lse, *(level_shift(run_lse, shift) for shift in range(1, SPAN))),
+        [SMEM] * 2 + [VMEM] * 4,
+        [((3, OWNERS, ROWS), f32)],
+        name="lse",
+    )
+    grad_query, grad_key, grad_value, first_sum, first_value = call(
+        first_kernel,
+        (where, table, query_side, key_side, first, given),
+        [SMEM] * 2 + [VMEM] * 4,
+        [(side, f32)] * 5,
+        rows,
+        flops=cost,
+        name="first",
+    )
+    grad_key, grad_value, query_sum, late_back, key_back = call(
+        second_kernel,
+        (where, table, key_side, first, second, given, grad_key, grad_value, first_sum, first_value),
+        [SMEM] * 2 + [VMEM] * 8,
+        [(side, f32)] * 3 + [(side, bf16), ((2,) + side, bf16)],
+        [pltpu.VMEM(side, f32), pltpu.VMEM(side, f32)] + rows,
+        flops=cost,
+        name="second",
+    )
+    key_back = swapped(key_back, mirror, mirror, (2, 3))
+    grad_key, grad_value, query_back = call(
+        third_kernel,
+        (where, table, key_side, second, grad_key, grad_value, query_sum),
+        [SMEM] * 2 + [VMEM] * 5,
+        [(side, f32)] * 2 + [(side, bf16)],
+        [pltpu.VMEM(side, f32)] + rows,
+        flops=4 * cost,
+        name="third",
+    )
+    query_back = swapped(query_back, mate, mate)
+    late_back = swapped(late_back, None, mirror, (0, 1))
+    grad_query, grad_key, grad_value = call(
+        own_kernel,
+        (where, table, query_side, key_side, given, grad_query, grad_key, grad_value),
+        [SMEM] * 2 + [VMEM] * 6,
+        [(side, f32)] * 3,
+        rows,
+        flops=1,
+        moved=1,
+        name="own",
+    )
+    (joined,) = call(
+        join_kernel,
+        (table, grad_query, grad_key, grad_value, query_back, late_back, key_back),
+        [SMEM] + [VMEM] * 6,
+        [((SPAN, 2, 3 * ROWS, HEAD_DIM), bf16)],
+        name="join",
+    )
+    (turned,) = call(
+        turn_kernel,
+        (exchanged(joined, head_groups),),
+        [VMEM],
+        [((2, SPAN, 3 * ROWS, HEAD_DIM), bf16)],
+        name="turn",
+    )
+    returned = exchanged(turned, core_groups)
+
+    def rising():
+        return tuple(
+            call(
+                unpack_kernel,
+                (returned,),
+                [VMEM],
+                [((ROWS, HEADS * HEAD_DIM), bf16)] * 3,
+                [pltpu.SemaphoreType.DMA((3, HEADS))],
+                name="unpack",
+                spaces=[HBM] * 3,
+            )
+        )
+
+    def falling():
+        return any_order(
+            queries, key_rows, value_rows, attn_output, grad_output, logsumexp, positions
+        )
+
+    first_places = lax.slice(positions, (0,), positions.shape, (OWNERS * ROWS,))
+    return lax.cond(jnp.any(first_places >= SPAN * 2 * CHUNK), falling, rising)
+
+
 def solution(mesh):
-    placed = (
-        P(("blk", "ulysses"), None),
-        P(("blk", "ulysses"), None),
-        P(("blk", "ulysses"), None),
-        P(("blk", "ulysses"), None),
-        P(("blk", "ulysses"), None),
-        P("blk", "ulysses"),
-        P(),
-    )
+    tokens = P(("blk", "ulysses"), None)
     return jax.shard_map(
         per_device,
         mesh=mesh,
-        in_specs=placed,
-        out_specs=(
-            P(("blk", "ulysses"), None),
-            P(("blk", "ulysses"), None),
-            P(("blk", "ulysses"), None),
-        ),
+        in_specs=(tokens,) * 5 + (P("blk", "ulysses"), P()),
+        out_specs=(tokens,) * 3,
         check_vma=False,
     )

time: 268 us -> 103 us (0.38)
  starting transfers between devices: 89.2 us -> 19.2 us
  matrix products: 61.2 us -> 0 us
  waiting for transfers between devices: 77.7 us -> 16.6 us
  blocking collectives: 0 us -> 44.3 us
  local copies, waits for them, and re-layouts: 26.9 us -> 1.2 us
  Pallas kernels: 0 us -> 17.7 us
  other arithmetic: 8.48 us -> 0.64 us
    dot_general x40 -> x0, matrix products: 61.2 us -> none  [the longest x8 13.8 us: tile_grads(): jnp.einsum('hqk,khd->qhd', grad_scores, key_tile, preferred_element_type=...]
    all_to_all x8 -> x1, waiting for transfers between devices: 61.9 us -> 9.61 us  [exchanged(): lax.all_to_all(value, AXES, split_axis=0, concat_axis=0, axis_index_group...]
    all_to_all x0 -> x3, blocking collectives: none -> 44.3 us  [exchanged(): lax.all_to_all(value, AXES, split_axis=0, concat_axis=0, axis_index_group...]
    all_to_all x8 -> x1, starting transfers between devices: 40.9 us -> 4.57 us  [exchanged(): lax.all_to_all(value, AXES, split_axis=0, concat_axis=0, axis_index_group...]
    ppermute x16 -> x8, starting transfers between devices: 48.3 us -> 14.6 us  [the longest x5 12.7 us: swapped(): return lax.ppermute(value, AXES, pairs)]
    pallas_call x0 -> x11, Pallas kernels: none -> 17.7 us  [call(): pl.pallas_call(kernel, out_shape=[jax.ShapeDtypeStruct(shape, dtype) for...]
    ppermute x16 -> x8, waiting for transfers between devices: 15.8 us -> 6.96 us  [the longest x5 6.95 us: swapped(): return lax.ppermute(value, AXES, pairs)]
    unnamed x28 -> x12, local copies, waits for them, and re-layouts: 8.79 us -> 0.03 us
  transfers between devices with their start and end apart: 24 -> 9, of which waited for: 10 -> 4; matrix products, arithmetic and copies ran while one was open for 33% -> 2% of each run, Pallas kernels for 0% -> 8%
where the time goes in v3:
time: 103 us; the launch traced here: 101 us
  blocking collectives  44.3 us (43%)
  starting transfers between devices  19.2 us (19%)
  Pallas kernels  17.7 us (17%)
  waiting for transfers between devices  16.6 us (16%)
  between operations  1.71 us (2%)
  local copies, waits for them, and re-layouts  1.2 us (1%)
    all_to_all x3, blocking collectives, exchanged(): lax.all_to_all(value, AXES, split_axis=0, concat_axis=0, axis_index_group...  44.3 us
    pallas_call x11, Pallas kernels, call(): pl.pallas_call(kernel, out_shape=[jax.ShapeDtypeStruct(shape, dtype) for...  17.7 us
    ppermute x5, starting transfers between devices, swapped(): return lax.ppermute(value, AXES, pairs)  12.7 us
    all_to_all x1, waiting for transfers between devices, exchanged(): lax.all_to_all(value, AXES, split_axis=0, concat_axis=0, axis_index_group...  9.61 us
    ppermute x5, waiting for transfers between devices, swapped(): return lax.ppermute(value, AXES, pairs)  6.95 us
    all_to_all x1, starting transfers between devices, exchanged(): lax.all_to_all(value, AXES, split_axis=0, concat_axis=0, axis_index_group...  4.57 us
  transfers between devices with their start and end apart: 9, of which 4 were waited for; matrix products, arithmetic and copies ran while one was open for 2% of the time, Pallas kernels for 8%

profile of v3, /device:TPU:56, one launch (start us, length us, event | category | flops | bytes accessed | tf_op | source)
XLA Modules:
  0.0 101.3 jit_solution(9415993191759667185)
XLA Ops:
  0.7 0.1 stack.19.where_ref
  0.8 3.5 %pack.1 = (bf16[2,4,528,128]{3,2,1,0:T(8,128)(2,1)S(1)}, s32[20]{0:T(128)S(1)}) custom-call(s32[5]{0:T(128)S(1)} %stack.19.where_ref, bf16[128,1024]{1,0:T(8,128)(2,1)} %query_ref.1, bf16[128,1024]{1,0:T(8,128)(2,1)} %key_ref.1, bf16[128,1024]{1,0:T(8,128)(2,1)} %value_ref.1, bf16[128,1024]{1,0:T(8,128)(2,1)} %output_ref.1, bf16[128,1024]{1,0:T(8,128)(2,1)} %cotangent_ref.1, ...), custom_call_target="tpu_custom_call" | custom-call | bytes 4194304 | tf_op jit(solution)/shard_map/pack/pallas_call | solution.py:476
  4.3 4.6 %all_to_all.127.moved_ref = bf16[2,4,528,128]{3,2,1,0:T(8,128)(2,1)S(1)} all-to-all(bf16[2,4,528,128]{3,2,1,0:T(8,128)(2,1)S(1)} %get-tuple-element.305), channel_id=1, replica_groups={{0,64},{1,65},{2,66},{3,67},{4,68},{5,69},{6,70},{7,71},{8,72},{9,73},{..., dimensions={0} | all-to-all | bytes 2162688 | tf_op jit(solution)/shard_map/all_to_all | solution.py:678
  8.9 0.1 arrange.1
  9.0 31.2 %all_to_all.128.slots_ref = bf16[4,2,528,128]{3,2,1,0:T(8,128)(2,1)S(1)} all-to-all(bf16[4,2,528,128]{3,2,1,0:T(8,128)(2,1)S(1)} %arrange.1), channel_id=1, replica_groups={{0,128,256,384},{1,129,257,385},{2,130,258,386},{3,131,259,387},{4,132,..., dimensions={0} | all-to-all | bytes 2162688 | tf_op jit(solution)/shard_map/all_to_all | solution.py:678
  40.1 0.7 split.1
  40.8 4.3 %collective-permute-start.19 = (bf16[8,272,128]{2,1,0:T(8,128)(2,1)S(1)}, bf16[8,272,128]{2,1,0:T(8,128)(2,1)S(1)}, u32[]{:S(2)}, u32[]{:S(2)}) collective-permute-start(bf16[8,272,128]{2,1,0:T(8,128)(2,1)S(1)} %get-tuple-element.309), channel_id=1, source_target_pairs={{0,48},{64,192},{1,49},{65,193},{2,50},{66,194},{3,51},{67,195},{4... | collective-permute-start | bytes 1671176 | tf_op jit(solution)/shard_map/ppermute | solution.py:655
  45.2 2.2 %collective-permute-start.20 = (bf16[8,272,128]{2,1,0:T(8,128)(2,1)S(1)}, bf16[8,272,128]{2,1,0:T(8,128)(2,1)S(1)}, u32[]{:S(2)}, u32[]{:S(2)}) collective-permute-start(bf16[8,272,128]{2,1,0:T(8,128)(2,1)S(1)} %get-tuple-element.311), channel_id=1, source_target_pairs={{0,16},{64,448},{1,17},{65,449},{2,18},{66,450},{3,19},{67,451},{4... | collective-permute-start | bytes 1671176 | tf_op jit(solution)/shard_map/ppermute | solution.py:655
  47.4 0.7 collective-permute-start.16
  48.1 0.7 collective-permute-start.17
  48.7 0.7 collective-permute-start.18
  49.4 0.6 lse.1.given_ref
  50.0 3.4 %collective-permute-done.19.first_ref = bf16[8,272,128]{2,1,0:T(8,128)(2,1)S(1)} collective-permute-done((bf16[8,272,128]{2,1,0:T(8,128)(2,1)S(1)}, bf16[8,272,128]{2,1,0:T(8,128)(2,1)S(1)}, u32[]{:S(2)}, u32[]{:S(2)}) %collective-permute-start.19) | collective-permute-done | bytes 557088 | tf_op jit(solution)/shard_map/ppermute | solution.py:655
  53.5 2.3 %first.1 = (f32[8,128,128]{2,1,0:T(8,128)S(1)}, f32[8,128,128]{2,1,0:T(8,128)S(1)}, f32[8,128,128]{2,1,0:T(8,128)S(1)}, f32[8,128,128]{2,1,0:T(8,128)S(1)}, f32[8,128,128]{2,1,0:T(8,128)S(1)}) custom-call(s32[5]{0:T(128)S(1)} %stack.19.where_ref, s32[20]{0:T(128)S(1)} %get-tuple-element.304.table_ref, ...), custom_call_target="tpu_custom_call" | custom-call | flops 671088640 | bytes 4194304 | tf_op jit(solution)/shard_map/first/pallas_call | solution.py:476
  55.8 0.8 collective-permute-done.20.second_ref
  56.6 2.5 %second.1 = (f32[8,128,128]{2,1,0:T(8,128)S(1)}, f32[8,128,128]{2,1,0:T(8,128)S(1)}, f32[8,128,128]{2,1,0:T(8,128)S(1)}, bf16[8,128,128]{2,1,0:T(8,128)(2,1)S(1)}, bf16[2,8,128,128]{3,2,1,0:T(8,128)(2,1)S(1)}) custom-call(s32[5]{0:T(128)S(1)} %stack.19.where_ref, s32[20]{0:T(128)S(1)} %get-tuple-element.304.table_ref, ...), custom_call_target="tpu_custom_call" | custom-call | flops 671088640 | bytes 4194304 | tf_op jit(solution)/shard_map/second/pallas_call | solution.py:476
  59.1 3.5 %collective-permute-start.23 = (bf16[2,8,128,128]{3,2,1,0:T(8,128)(2,1)S(1)}, bf16[2,8,128,128]{3,2,1,0:T(8,128)(2,1)S(1)}, u32[]{:S(2)}, u32[]{:S(2)}) collective-permute-start(bf16[2,8,128,128]{3,2,1,0:T(8,128)(2,1)S(1)} %get-tuple-element.326), channel_id=1, source_target_pairs={{0,48},{1,49},{2,50},{3,51},{4,52},{5,53},{6,54},{7,55},{72,120},{... | collective-permute-start | bytes 1572872 | tf_op jit(solution)/shard_map/ppermute | solution.py:655
  62.6 2.3 %third.1 = (f32[8,128,128]{2,1,0:T(8,128)S(1)}, f32[8,128,128]{2,1,0:T(8,128)S(1)}, bf16[8,128,128]{2,1,0:T(8,128)(2,1)S(1)}) custom-call(s32[5]{0:T(128)S(1)} %stack.19.where_ref, s32[20]{0:T(128)S(1)} %get-tuple-element.304.table_ref, bf16[8,272,128]{2,1,0:T(8,128)(2,1)S(1)} %get-tuple-element.307.key_side_ref, ...), custom_call_target="tpu_custom_call" | custom-call | flops 2684354560 | bytes 4194304 | tf_op jit(solution)/shard_map/third/pallas_call | solution.py:476
  64.9 1.9 %collective-permute-start.21 = (bf16[8,128,128]{2,1,0:T(8,128)(2,1)S(1)}, bf16[8,128,128]{2,1,0:T(8,128)(2,1)S(1)}, u32[]{:S(2)}, u32[]{:S(2)}) collective-permute-start(bf16[8,128,128]{2,1,0:T(8,128)(2,1)S(1)} %get-tuple-element.324), channel_id=1, source_target_pairs={{0,16},{64,192},{1,17},{65,193},{2,18},{66,194},{3,19},{67,195},{4... | collective-permute-start | bytes 786440 | tf_op jit(solution)/shard_map/ppermute | solution.py:655
  66.8 0.7 collective-permute-start.22
  67.5 3.0 %own.1 = (f32[8,128,128]{2,1,0:T(8,128)S(1)}, f32[8,128,128]{2,1,0:T(8,128)S(1)}, f32[8,128,128]{2,1,0:T(8,128)S(1)}) custom-call(s32[5]{0:T(128)S(1)} %stack.19.where_ref, s32[20]{0:T(128)S(1)} %get-tuple-element.304.table_ref, bf16[8,272,128]{2,1,0:T(8,128)(2,1)S(1)} %get-tuple-element.306.query_side_ref, ...), custom_call_target="tpu_custom_call" | custom-call | flops 1 | bytes 1 | tf_op jit(solution)/shard_map/own/pallas_call | solution.py:476
  70.4 2.7 %collective-permute-done.21.query_back_ref = bf16[8,128,128]{2,1,0:T(8,128)(2,1)S(1)} collective-permute-done((bf16[8,128,128]{2,1,0:T(8,128)(2,1)S(1)}, bf16[8,128,128]{2,1,0:T(8,128)(2,1)S(1)}, u32[]{:S(2)}, u32[]{:S(2)}) %collective-permute-start.21) | collective-permute-done | bytes 262176 | tf_op jit(solution)/shard_map/ppermute | solution.py:655
  73.2 1.7 %join.1 = bf16[4,2,384,128]{3,2,1,0:T(8,128)(2,1)} custom-call(s32[20]{0:T(128)S(1)} %get-tuple-element.304.table_ref, f32[8,128,128]{2,1,0:T(8,128)S(1)} %get-tuple-element.321.grad_query_ref, f32[8,128,128]{2,1,0:T(8,128)S(1)} %get-tuple-element.322.grad_key_ref, f32[8,128,128]{2,1,0:T(8,128)S(1)} %get-tuple-element.323.grad_value_ref, ...), custom_call_target="tpu_custom_call" | custom-call | bytes 4194304 | tf_op jit(solution)/shard_map/join/pallas_call | solution.py:476
  74.8 0.0 copy-start.30
  74.9 4.6 %all-to-all-start.10 = ((bf16[4,2,384,128]{3,2,1,0:T(8,128)(2,1)}), bf16[4,2,384,128]{3,2,1,0:T(8,128)(2,1)S(1)}, u32[]{:S(2)}, u32[]{:S(2)}) async-start(bf16[4,2,384,128]{3,2,1,0:T(8,128)(2,1)} %join.1), calls=%async_computation.10 | async-start | bytes 1572864 | tf_op jit(solution)/shard_map/all_to_all | solution.py:678
  79.4 1.1 %slice.3 = s32[64]{0:T(128)S(1)} slice(s32[65536]{0:T(1024)} %positions_ref.1), slice={[0:65536:1024]} | slice | bytes 512 | tf_op jit(solution)/shard_map/slice | solution.py:802
  80.5 0.6 compare_reduce_fusion
  81.8 9.6 %all-to-all-done.10.slots_ref = bf16[4,2,384,128]{3,2,1,0:T(8,128)(2,1)S(1)} async-done(((bf16[4,2,384,128]{3,2,1,0:T(8,128)(2,1)}), bf16[4,2,384,128]{3,2,1,0:T(8,128)(2,1)S(1)}, u32[]{:S(2)}, u32[]{:S(2)}) %all-to-all-start.10) | async-done | bytes 786464 | tf_op jit(solution)/shard_map/all_to_all | solution.py:678
  91.4 0.1 turn.1
  91.5 8.5 %all_to_all.129 = bf16[2,4,384,128]{3,2,1,0:T(8,128)(2,1)S(1)} all-to-all(bf16[2,4,384,128]{3,2,1,0:T(8,128)(2,1)S(1)} %turn.1), channel_id=1, replica_groups={{0,64},{1,65},{2,66},{3,67},{4,68},{5,69},{6,70},{7,71},{8,72},{9,73},{..., dimensions={0} | all-to-all | bytes 1572864 | tf_op jit(solution)/shard_map/all_to_all | solution.py:678
  100.0 1.1 %conditional.1 = ((bf16[128,1024]{1,0:T(8,128)(2,1)}, bf16[128,1024]{1,0:T(8,128)(2,1)}, bf16[128,1024]{1,0:T(8,128)(2,1)})) conditional(s32[]{:T(128)} %convert_element_type.73, bf16[2,4,384,128]{3,2,1,0:T(8,128)(2,1)S(1)} %all_to_all.129, (bf16[128,1024]{1,0:T(8,128)(2,1)S(1)}, bf16[128,1024]{1,0:T(8,128)(2,1)S(1)}, s32[65536]{0:T(1024)}, ...), branch_computations={%region_1.2_spmd, %region_2.12_spmd} | conditional | flops 2704931840 | bytes 142573088 | solution.py:803
  100.0 1.1 %unpack.1 = (bf16[128,1024]{1,0:T(8,128)(2,1)}, bf16[128,1024]{1,0:T(8,128)(2,1)}, bf16[128,1024]{1,0:T(8,128)(2,1)}) custom-call(bf16[2,4,384,128]{3,2,1,0:T(8,128)(2,1)S(1)} %moved_ref), custom_call_target="tpu_custom_call" | custom-call | bytes 4194304 | tf_op jit(solution)/shard_map/cond/branch_0_fun/unpack/pallas_call | solution.py:476
  (16 shorter events, 0.0 us)
Async XLA Ops:
  0.6 8.3 %copy-start.31 = (f32[1024,1]{0,1:T(1,128)S(1)}, f32[1024,1]{0,1:T(1,128)}, u32[]{:S(2)}) copy-start(f32[1024,1]{0,1:T(1,128)} %param.22) | copy-start | bytes 12292
  40.8 12.6 %collective-permute-start.19 = (bf16[8,272,128]{2,1,0:T(8,128)(2,1)S(1)}, bf16[8,272,128]{2,1,0:T(8,128)(2,1)S(1)}, u32[]{:S(2)}, u32[]{:S(2)}) collective-permute-start(bf16[8,272,128]{2,1,0:T(8,128)(2,1)S(1)} %get-tuple-element.309), channel_id=1, source_target_pairs={{0,48},{64,192},{1,49},{65,193},{2,50},{66,194},{3,51},{67,195},{4... | collective-permute-start | bytes 1671176 | tf_op jit(solution)/shard_map/ppermute | solution.py:655
  45.2 11.4 %collective-permute-start.20 = (bf16[8,272,128]{2,1,0:T(8,128)(2,1)S(1)}, bf16[8,272,128]{2,1,0:T(8,128)(2,1)S(1)}, u32[]{:S(2)}, u32[]{:S(2)}) collective-permute-start(bf16[8,272,128]{2,1,0:T(8,128)(2,1)S(1)} %get-tuple-element.311), channel_id=1, source_target_pairs={{0,16},{64,448},{1,17},{65,449},{2,18},{66,450},{3,19},{67,451},{4... | collective-permute-start | bytes 1671176 | tf_op jit(solution)/shard_map/ppermute | solution.py:655
  47.4 2.0 %collective-permute-start.16 = (f32[4,8,128]{2,1,0:T(8,128)S(1)}, f32[4,8,128]{2,1,0:T(8,128)S(1)}, u32[]{:S(2)}, u32[]{:S(2)}) collective-permute-start(f32[4,8,128]{2,1,0:T(8,128)S(1)} %get-tuple-element.308.run_lse_ref), channel_id=1, source_target_pairs={{64,192},{65,193},{66,194},{67,195},{68,196},{69,197},{70,198},{71... | collective-permute-start | bytes 49160 | tf_op jit(solution)/shard_map/ppermute | solution.py:666
  48.1 1.4 %collective-permute-start.17 = (f32[4,8,128]{2,1,0:T(8,128)S(1)}, f32[4,8,128]{2,1,0:T(8,128)S(1)}, u32[]{:S(2)}, u32[]{:S(2)}) collective-permute-start(f32[4,8,128]{2,1,0:T(8,128)S(1)} %get-tuple-element.308.run_lse_ref), channel_id=1, source_target_pairs={{64,320},{65,321},{66,322},{67,323},{68,324},{69,325},{70,326},{71... | collective-permute-start | bytes 49160 | tf_op jit(solution)/shard_map/ppermute | solution.py:666
  48.7 0.7 collective-permute-start.18
  59.1 14.1 %collective-permute-start.23 = (bf16[2,8,128,128]{3,2,1,0:T(8,128)(2,1)S(1)}, bf16[2,8,128,128]{3,2,1,0:T(8,128)(2,1)S(1)}, u32[]{:S(2)}, u32[]{:S(2)}) collective-permute-start(bf16[2,8,128,128]{3,2,1,0:T(8,128)(2,1)S(1)} %get-tuple-element.326), channel_id=1, source_target_pairs={{0,48},{1,49},{2,50},{3,51},{4,52},{5,53},{6,54},{7,55},{72,120},{... | collective-permute-start | bytes 1572872 | tf_op jit(solution)/shard_map/ppermute | solution.py:655
  64.9 8.3 %collective-permute-start.21 = (bf16[8,128,128]{2,1,0:T(8,128)(2,1)S(1)}, bf16[8,128,128]{2,1,0:T(8,128)(2,1)S(1)}, u32[]{:S(2)}, u32[]{:S(2)}) collective-permute-start(bf16[8,128,128]{2,1,0:T(8,128)(2,1)S(1)} %get-tuple-element.324), channel_id=1, source_target_pairs={{0,16},{64,192},{1,17},{65,193},{2,18},{66,194},{3,19},{67,195},{4... | collective-permute-start | bytes 786440 | tf_op jit(solution)/shard_map/ppermute | solution.py:655
  66.8 6.3 %collective-permute-start.22 = (bf16[8,128,128]{2,1,0:T(8,128)(2,1)S(1)}, bf16[8,128,128]{2,1,0:T(8,128)(2,1)S(1)}, u32[]{:S(2)}, u32[]{:S(2)}) collective-permute-start(bf16[8,128,128]{2,1,0:T(8,128)(2,1)S(1)} %get-tuple-element.325), channel_id=1, source_target_pairs={{64,448},{65,449},{66,450},{67,451},{68,452},{69,453},{70,454},{71... | collective-permute-start | bytes 786440 | tf_op jit(solution)/shard_map/ppermute | solution.py:655
  74.8 16.6 %copy-start.26 = (bf16[128,1024]{1,0:T(8,128)(2,1)S(1)}, bf16[128,1024]{1,0:T(8,128)(2,1)}, u32[]{:S(2)}) copy-start(bf16[128,1024]{1,0:T(8,128)(2,1)} %query_ref.1) | copy-start | bytes 786436
  74.8 16.7 %copy-start.27 = (bf16[128,1024]{1,0:T(8,128)(2,1)S(1)}, bf16[128,1024]{1,0:T(8,128)(2,1)}, u32[]{:S(2)}) copy-start(bf16[128,1024]{1,0:T(8,128)(2,1)} %key_ref.1) | copy-start | bytes 786436
  74.8 16.7 %copy-start.28 = (bf16[128,1024]{1,0:T(8,128)(2,1)S(1)}, bf16[128,1024]{1,0:T(8,128)(2,1)}, u32[]{:S(2)}) copy-start(bf16[128,1024]{1,0:T(8,128)(2,1)} %value_ref.1) | copy-start | bytes 786436
  74.8 16.7 %copy-start.29 = (bf16[128,1024]{1,0:T(8,128)(2,1)S(1)}, bf16[128,1024]{1,0:T(8,128)(2,1)}, u32[]{:S(2)}) copy-start(bf16[128,1024]{1,0:T(8,128)(2,1)} %output_ref.1) | copy-start | bytes 786436
  74.8 16.7 %copy-start.30 = (bf16[128,1024]{1,0:T(8,128)(2,1)S(1)}, bf16[128,1024]{1,0:T(8,128)(2,1)}, u32[]{:S(2)}) copy-start(bf16[128,1024]{1,0:T(8,128)(2,1)} %cotangent_ref.1) | copy-start | bytes 786436
  74.9 16.6 %all-to-all-start.10 = ((bf16[4,2,384,128]{3,2,1,0:T(8,128)(2,1)}), bf16[4,2,384,128]{3,2,1,0:T(8,128)(2,1)S(1)}, u32[]{:S(2)}, u32[]{:S(2)}) async-start(bf16[4,2,384,128]{3,2,1,0:T(8,128)(2,1)} %join.1), calls=%async_computation.10 | async-start | bytes 1572864 | tf_op jit(solution)/shard_map/all_to_all | solution.py:678

commit v4 on v3

--- a/solution.py
+++ b/solution.py
@@ -61,10 +61,11 @@
     for slot in range(SPAN):
         table_ref[12 + slot] = jnp.where(role == 0, slot, rank_at(level, pairs[slot]))
         table_ref[16 + slot] = pairs[slot]
+    for index, value in enumerate((role, place, level)):
+        table_ref[20 + index] = value
 
 
 def pack_kernel(
-    where_ref,
     query_ref,
     key_ref,
     value_ref,
@@ -78,7 +79,10 @@
     arrived,
     places_arrived,
 ):
-    role, place, level, line, stride = (where_ref[index] for index in range(5))
+    stride = lax.axis_size("blk") // SPAN
+    rank, here = lax.axis_index("ulysses"), lax.axis_index("blk")
+    place, line, level = lax.div(here, stride), lax.rem(here, stride), lax.div(rank, 2)
+    role = lax.rem(rank, 2) ^ lax.div(2 * line, stride)
     run_rows = OWNERS * ROWS
     first_places = []
     for run in range(SPAN):
@@ -99,11 +103,17 @@
 
     sources = (query_ref, cotangent_ref, key_ref, value_ref, output_ref)
     moves = [list(copies(index, source)) for index, source in enumerate(sources)]
+    for move in first_places:
+        move.start()
     for index in (1, 4, 0, 2, 3):
         for move in moves[index]:
             move.start()
     for move in first_places:
-        move.start()
+        move.wait()
+    pairs = [
+        jnp.minimum(lax.div(places[run, 0], jnp.int32(2 * CHUNK)), SPAN - 1) for run in range(SPAN)
+    ]
+    fill_table(table_ref, pairs, role, place, level)
     row = lax.broadcasted_iota(jnp.int32, (EXTRA, ROWS), 0)
     for head in range(HEADS):
         moves[1][head].wait()
@@ -113,12 +123,6 @@
         high, middle, low = three_terms(delta)
         rows = jnp.where(row == 0, high, jnp.where(row == 1, middle, jnp.where(row == 2, low, 0.0)))
         packed_ref[head % 2, head // 2, 512:528, :] = rows.astype(bf16)
-    for move in first_places:
-        move.wait()
-    pairs = [
-        jnp.minimum(lax.div(places[run, 0], jnp.int32(2 * CHUNK)), SPAN - 1) for run in range(SPAN)
-    ]
-    fill_table(table_ref, pairs, role, place, level)
     for index in (0, 2, 3):
         for move in moves[index]:
             move.wait()
@@ -142,7 +146,6 @@
 
 
 def split_kernel(
-    where_ref,
     table_ref,
     slots_ref,
     lse_ref,
@@ -152,7 +155,7 @@
     second_ref,
     run_lse_ref,
 ):
-    role, level = where_ref[0], where_ref[2]
+    role, level = table_ref[20], table_ref[22]
     for slot in range(SPAN):
         for owner in range(2):
             block = 2 * table_ref[12 + slot] + owner
@@ -187,9 +190,9 @@
         second_ref[...] = key_side_ref[...]
 
 
-def lse_kernel(where_ref, table_ref, run_lse_ref, *rest):
+def lse_kernel(table_ref, run_lse_ref, *rest):
     shifted_refs, given_ref = rest[:-1], rest[-1]
-    place, level = where_ref[1], where_ref[2]
+    place, level = table_ref[21], table_ref[22]
     shift = lax.rem(level - place + SPAN, SPAN)
 
     def fill(source_ref):
@@ -284,8 +287,8 @@
 
 
 def own_kernel(
-    where_ref,
     table_ref,
+    _,
     query_side_ref,
     key_side_ref,
     given_ref,
@@ -301,11 +304,11 @@
     grad_key_ref[...] = last_key_ref[...]
     grad_value_ref[...] = last_value_ref[...]
 
-    @pl.when(where_ref[0] == 0)
+    @pl.when(table_ref[20] == 0)
     def _():
         read_rows(query_side_ref, *rows)
 
-    @pl.when(where_ref[0] != 0)
+    @pl.when(table_ref[20] != 0)
     def _():
         read_rows(query_side_ref, *rows, (given_ref, 0))
 
@@ -314,7 +317,6 @@
 
 
 def first_kernel(
-    where_ref,
     table_ref,
     query_side_ref,
     key_side_ref,
@@ -330,13 +332,13 @@
     for ref in (grad_query_ref, grad_key_ref, grad_value_ref, first_sum_ref, first_value_ref):
         ref[...] = jnp.zeros_like(ref)
 
-    @pl.when(where_ref[0] == 0)
+    @pl.when(table_ref[20] == 0)
     def _():
         read_rows(query_side_ref, *rows)
         query_refs = (query_side_ref, *rows, grad_query_ref)
         paired_grads(table_ref, 0, 1, query_refs, (first_ref, first_sum_ref, first_value_ref))
 
-    @pl.when(where_ref[0] != 0)
+    @pl.when(table_ref[20] != 0)
     def _():
         read_rows(first_ref, *rows, (given_ref, 1))
         query_refs = (first_ref, *rows, first_sum_ref)
@@ -344,7 +346,6 @@
 
 
 def second_kernel(
-    where_ref,
     table_ref,
     key_side_ref,
     first_ref,
@@ -357,13 +358,12 @@
     grad_key_ref,
     grad_value_ref,
     query_sum_ref,
-    late_back_ref,
-    key_back_ref,
+    far_back_ref,
     key_sum,
     value_sum,
     *rows,
 ):
-    role, level = where_ref[0], where_ref[2]
+    role, level = table_ref[20], table_ref[22]
     grad_key_ref[...] = last_key_ref[...]
     grad_value_ref[...] = last_value_ref[...]
 
@@ -387,7 +387,10 @@
         read_rows(second_ref, *rows, (given_ref, 2))
         query_refs = (second_ref, *rows, key_sum)
         whole_grads(query_refs, (key_side_ref, grad_key_ref, grad_value_ref))
-        late_back_ref[...] = (key_sum[...] * SCALE).astype(bf16)
+        total = key_sum[...] * SCALE
+        high = total.astype(bf16)
+        far_back_ref[0] = high
+        far_back_ref[1] = (total - high.astype(f32)).astype(bf16)
 
     @pl.when((role != 0) & (level > 1))
     def _():
@@ -397,12 +400,11 @@
 
     @pl.when((role == 0) | (level > 1))
     def _():
-        key_back_ref[0] = (key_sum[...] * SCALE).astype(bf16)
-        key_back_ref[1] = value_sum[...].astype(bf16)
+        far_back_ref[0] = (key_sum[...] * SCALE).astype(bf16)
+        far_back_ref[1] = value_sum[...].astype(bf16)
 
 
 def third_kernel(
-    where_ref,
     table_ref,
     key_side_ref,
     second_ref,
@@ -419,7 +421,7 @@
     grad_value_ref[...] = last_value_ref[...]
     query_sum[...] = last_sum_ref[...]
 
-    @pl.when(where_ref[0] == 0)
+    @pl.when(table_ref[20] == 0)
     def _():
         read_rows(second_ref, *rows)
         query_refs = (second_ref, *rows, query_sum)
@@ -429,23 +431,18 @@
 
 
 def join_kernel(
-    table_ref,
-    grad_query_ref,
-    grad_key_ref,
-    grad_value_ref,
-    query_back_ref,
-    late_back_ref,
-    key_back_ref,
-    slots_ref,
+    table_ref, grad_query_ref, grad_key_ref, grad_value_ref, query_back_ref, far_back_ref, slots_ref
 ):
+    to_query = jnp.where((table_ref[20] != 0) & (table_ref[22] > 1), 1.0, 0.0).astype(f32)
     for slot in range(SPAN):
         for owner in range(2):
             at = 2 * table_ref[12 + slot] + owner
-            back = query_back_ref[at].astype(f32) + late_back_ref[at].astype(f32)
+            back = query_back_ref[at].astype(f32)
+            one, two = far_back_ref[0, at].astype(f32), far_back_ref[1, at].astype(f32)
             sums = (
-                grad_query_ref[at] * SCALE + back,
-                grad_key_ref[at] * SCALE + key_back_ref[0, at].astype(f32),
-                grad_value_ref[at] + key_back_ref[1, at].astype(f32),
+                grad_query_ref[at] * SCALE + back + to_query * (one + two),
+                grad_key_ref[at] * SCALE + (1.0 - to_query) * one,
+                grad_value_ref[at] + (1.0 - to_query) * two,
             )
             for index, total in enumerate(sums):
                 slots_ref[slot, owner, index * ROWS : (index + 1) * ROWS, :] = total.astype(bf16)
@@ -634,24 +631,17 @@
 def per_device(queries, key_rows, value_rows, attn_output, grad_output, logsumexp, positions):
     blk_count = lax.axis_size("blk")
     stride = blk_count // SPAN
-    rank, here = lax.axis_index("ulysses"), lax.axis_index("blk")
-    line = here % stride
-    role = (rank % 2) ^ (2 * line // stride)
-    where = jnp.stack([role, here // stride, rank // 2, line, jnp.int32(stride)])
-
     def index_of(role, place, level, at):
         core = role ^ (2 * at // stride)
         return (2 * level + core) * blk_count + place * stride + at
 
     spots = [(p, z, at) for p in range(SPAN) for z in range(SPAN) for at in range(stride)]
 
-    def swapped(value, over_x, over_z, levels=range(SPAN)):
+    def swapped(value, over_x, over_z):
         pairs = []
         for p, z, at in spots:
-            if over_x is not None:
-                pairs.append((index_of(0, p, z, at), index_of(0, over_x(p), z, at)))
-            if z in levels:
-                pairs.append((index_of(1, p, z, at), index_of(1, p, over_z(z), at)))
+            pairs.append((index_of(0, p, z, at), index_of(0, over_x(p), z, at)))
+            pairs.append((index_of(1, p, z, at), index_of(1, p, over_z(z), at)))
         return lax.ppermute(value, AXES, pairs)
 
     mate = lambda at: at ^ 1
@@ -687,9 +677,9 @@
     ]
     packed, table = call(
         pack_kernel,
-        (where, *tokens),
-        [SMEM] + [HBM] * 6,
-        [((2, SPAN, PART, HEAD_DIM), bf16), ((20,), jnp.int32)],
+        tokens,
+        [HBM] * 6,
+        [((2, SPAN, PART, HEAD_DIM), bf16), ((24,), jnp.int32)],
         [
             pltpu.VMEM((HEADS, ROWS, HEAD_DIM), bf16),
             pltpu.SMEM((SPAN, 128), jnp.int32),
@@ -710,54 +700,56 @@
     rows = [row_scratch(), row_scratch()]
     query_side, key_side, first_out, second_out, run_lse = call(
         split_kernel,
-        (where, table, exchanged(slots, head_groups), lse),
-        [SMEM] * 2 + [VMEM] * 2,
+        (table, exchanged(slots, head_groups), lse),
+        [SMEM] + [VMEM] * 2,
         [card] * 4 + [((SPAN, OWNERS, ROWS), f32)],
         name="split",
     )
     first = swapped(first_out, mirror, mate)
     second = swapped(second_out, mate, mirror)
     cost = 10 * 128 * 2 * 512 * 512
+    late_positions, _ = lax.optimization_barrier((positions, run_lse))
+    first_places = lax.slice(late_positions, (0,), positions.shape, (OWNERS * ROWS,))
+    flag = jnp.max(first_places).reshape(1)
     (given,) = call(
         lse_kernel,
-        (where, table, run_lse, *(level_shift(run_lse, shift) for shift in range(1, SPAN))),
-        [SMEM] * 2 + [VMEM] * 4,
+        (table, run_lse, *(level_shift(run_lse, shift) for shift in range(1, SPAN))),
+        [SMEM] + [VMEM] * 4,
         [((3, OWNERS, ROWS), f32)],
         name="lse",
     )
     grad_query, grad_key, grad_value, first_sum, first_value = call(
         first_kernel,
-        (where, table, query_side, key_side, first, given),
-        [SMEM] * 2 + [VMEM] * 4,
+        (table, query_side, key_side, first, given),
+        [SMEM] + [VMEM] * 4,
         [(side, f32)] * 5,
         rows,
         flops=cost,
         name="first",
     )
-    grad_key, grad_value, query_sum, late_back, key_back = call(
+    grad_key, grad_value, query_sum, far_back = call(
         second_kernel,
-        (where, table, key_side, first, second, given, grad_key, grad_value, first_sum, first_value),
-        [SMEM] * 2 + [VMEM] * 8,
-        [(side, f32)] * 3 + [(side, bf16), ((2,) + side, bf16)],
+        (table, key_side, first, second, given, grad_key, grad_value, first_sum, first_value),
+        [SMEM] + [VMEM] * 8,
+        [(side, f32)] * 3 + [((2,) + side, bf16)],
         [pltpu.VMEM(side, f32), pltpu.VMEM(side, f32)] + rows,
         flops=cost,
         name="second",
     )
-    key_back = swapped(key_back, mirror, mirror, (2, 3))
+    far_back = swapped(far_back, mirror, mirror)
     grad_key, grad_value, query_back = call(
         third_kernel,
-        (where, table, key_side, second, grad_key, grad_value, query_sum),
-        [SMEM] * 2 + [VMEM] * 5,
+        (table, key_side, second, grad_key, grad_value, query_sum),
+        [SMEM] + [VMEM] * 5,
         [(side, f32)] * 2 + [(side, bf16)],
         [pltpu.VMEM(side, f32)] + rows,
         flops=4 * cost,
         name="third",
     )
     query_back = swapped(query_back, mate, mate)
-    late_back = swapped(late_back, None, mirror, (0, 1))
     grad_query, grad_key, grad_value = call(
         own_kernel,
-        (where, table, query_side, key_side, given, grad_query, grad_key, grad_value),
+        (table, flag, query_side, key_side, given, grad_query, grad_key, grad_value),
         [SMEM] * 2 + [VMEM] * 6,
         [(side, f32)] * 3,
         rows,
@@ -765,27 +757,25 @@
         moved=1,
         name="own",
     )
-    (joined,) = call(
-        join_kernel,
-        (table, grad_query, grad_key, grad_value, query_back, late_back, key_back),
-        [SMEM] + [VMEM] * 6,
-        [((SPAN, 2, 3 * ROWS, HEAD_DIM), bf16)],
-        name="join",
-    )
-    (turned,) = call(
-        turn_kernel,
-        (exchanged(joined, head_groups),),
-        [VMEM],
-        [((2, SPAN, 3 * ROWS, HEAD_DIM), bf16)],
-        name="turn",
-    )
-    returned = exchanged(turned, core_groups)
-
     def rising():
+        (joined,) = call(
+            join_kernel,
+            (table, grad_query, grad_key, grad_value, query_back, far_back),
+            [SMEM] + [VMEM] * 5,
+            [((SPAN, 2, 3 * ROWS, HEAD_DIM), bf16)],
+            name="join",
+        )
+        (turned,) = call(
+            turn_kernel,
+            (exchanged(joined, head_groups),),
+            [VMEM],
+            [((2, SPAN, 3 * ROWS, HEAD_DIM), bf16)],
+            name="turn",
+        )
         return tuple(
             call(
                 unpack_kernel,
-                (returned,),
+                (exchanged(turned, core_groups),),
                 [VMEM],
                 [((ROWS, HEADS * HEAD_DIM), bf16)] * 3,
                 [pltpu.SemaphoreType.DMA((3, HEADS))],
@@ -799,8 +789,7 @@
             queries, key_rows, value_rows, attn_output, grad_output, logsumexp, positions
         )
 
-    first_places = lax.slice(positions, (0,), positions.shape, (OWNERS * ROWS,))
-    return lax.cond(jnp.any(first_places >= SPAN * 2 * CHUNK), falling, rising)
+    return lax.cond(flag[0] >= SPAN * 2 * CHUNK, falling, rising)
 
 
 def solution(mesh):

time: 103 us -> 99.7 us (0.968)
  blocking collectives: 44.3 us -> 58.6 us
  waiting for transfers between devices: 16.6 us -> 4.77 us
  starting transfers between devices: 19.2 us -> 14 us
    all_to_all x3 -> x4, blocking collectives: 44.3 us -> 58.6 us  [exchanged(): lax.all_to_all(value, AXES, split_axis=0, concat_axis=0, axis_index_group...]
    all_to_all x1 -> x0, waiting for transfers between devices: 9.61 us -> none  [exchanged(): lax.all_to_all(value, AXES, split_axis=0, concat_axis=0, axis_index_group...]
    all_to_all x1 -> x0, starting transfers between devices: 4.57 us -> none  [exchanged(): lax.all_to_all(value, AXES, split_axis=0, concat_axis=0, axis_index_group...]
    ppermute x5 -> x4, waiting for transfers between devices: 6.95 us -> 4.76 us  [swapped(): return lax.ppermute(value, AXES, pairs)]
    ppermute x5 -> x4, starting transfers between devices: 12.7 us -> 12 us  [swapped(): return lax.ppermute(value, AXES, pairs)]
  transfers between devices with their start and end apart: 9 -> 7, of which waited for: 4 -> 3; matrix products, arithmetic and copies ran while one was open for 2% -> 2% of each run, Pallas kernels for 8% -> 9%
where the time goes in v4:
time: 99.7 us; the launch traced here: 98.1 us
  blocking collectives  58.6 us (59%)
  Pallas kernels  17.4 us (17%)
  starting transfers between devices  14 us (14%)
  waiting for transfers between devices  4.77 us (5%)
  between operations  1.59 us (2%)
  local copies, waits for them, and re-layouts  1.1 us (1%)
    all_to_all x4, blocking collectives, exchanged(): lax.all_to_all(value, AXES, split_axis=0, concat_axis=0, axis_index_group...  58.6 us
    pallas_call x11, Pallas kernels, call(): pl.pallas_call(kernel, out_shape=[jax.ShapeDtypeStruct(shape, dtype) for...  17.4 us
    ppermute x4, starting transfers between devices, swapped(): return lax.ppermute(value, AXES, pairs)  12 us
    ppermute x4, waiting for transfers between devices, swapped(): return lax.ppermute(value, AXES, pairs)  4.76 us
  transfers between devices with their start and end apart: 7, of which 3 were waited for; matrix products, arithmetic and copies ran while one was open for 2% of the time, Pallas kernels for 9%

profile of v4, /device:TPU:56, one launch (start us, length us, event | category | flops | bytes accessed | tf_op | source)
XLA Modules:
  0.0 98.1 jit_solution(17032625011383635976)
XLA Ops:
  0.6 2.9 %pack.1 = (bf16[2,4,528,128]{3,2,1,0:T(8,128)(2,1)S(1)}, s32[24]{0:T(128)S(1)}) custom-call(bf16[128,1024]{1,0:T(8,128)(2,1)} %query_ref.1, bf16[128,1024]{1,0:T(8,128)(2,1)} %key_ref.1, bf16[128,1024]{1,0:T(8,128)(2,1)} %value_ref.1, bf16[128,1024]{1,0:T(8,128)(2,1)} %output_ref.1, bf16[128,1024]{1,0:T(8,128)(2,1)} %cotangent_ref.1, s32[65536]{0:T(1024)} %positions_ref.1), custom_call_target="tpu_custom_call" | custom-call | bytes 4194304 | tf_op jit(solution)/shard_map/pack/pallas_call | solution.py:473
  3.6 4.6 %all_to_all.124.moved_ref = bf16[2,4,528,128]{3,2,1,0:T(8,128)(2,1)S(1)} all-to-all(bf16[2,4,528,128]{3,2,1,0:T(8,128)(2,1)S(1)} %get-tuple-element.322), channel_id=1, replica_groups={{0,64},{1,65},{2,66},{3,67},{4,68},{5,69},{6,70},{7,71},{8,72},{9,73},{..., dimensions={0} | all-to-all | bytes 2162688 | tf_op jit(solution)/shard_map/all_to_all | solution.py:668
  8.2 0.1 arrange.1
  8.2 31.2 %all_to_all.125.slots_ref = bf16[4,2,528,128]{3,2,1,0:T(8,128)(2,1)S(1)} all-to-all(bf16[4,2,528,128]{3,2,1,0:T(8,128)(2,1)S(1)} %arrange.1), channel_id=1, replica_groups={{0,128,256,384},{1,129,257,385},{2,130,258,386},{3,131,259,387},{4,132,..., dimensions={0} | all-to-all | bytes 2162688 | tf_op jit(solution)/shard_map/all_to_all | solution.py:668
  39.4 0.7 split.1
  40.1 4.3 %collective-permute-start.19 = (bf16[8,272,128]{2,1,0:T(8,128)(2,1)S(1)}, bf16[8,272,128]{2,1,0:T(8,128)(2,1)S(1)}, u32[]{:S(2)}, u32[]{:S(2)}) collective-permute-start(bf16[8,272,128]{2,1,0:T(8,128)(2,1)S(1)} %get-tuple-element.327), channel_id=1, source_target_pairs={{0,48},{64,192},{1,49},{65,193},{2,50},{66,194},{3,51},{67,195},{4... | collective-permute-start | bytes 1671176 | tf_op jit(solution)/shard_map/ppermute | solution.py:645
  44.4 2.2 %collective-permute-start.20 = (bf16[8,272,128]{2,1,0:T(8,128)(2,1)S(1)}, bf16[8,272,128]{2,1,0:T(8,128)(2,1)S(1)}, u32[]{:S(2)}, u32[]{:S(2)}) collective-permute-start(bf16[8,272,128]{2,1,0:T(8,128)(2,1)S(1)} %get-tuple-element.329), channel_id=1, source_target_pairs={{0,16},{64,448},{1,17},{65,449},{2,18},{66,450},{3,19},{67,451},{4... | collective-permute-start | bytes 1671176 | tf_op jit(solution)/shard_map/ppermute | solution.py:645
  46.7 0.7 collective-permute-start.16
  47.3 0.7 collective-permute-start.17
  48.0 0.7 collective-permute-start.18
  48.7 0.0 collective-permute-done.16.rest_0_
  48.7 0.0 collective-permute-done.17.rest_1_
  48.7 0.0 collective-permute-done.18.rest_2_
  48.7 0.6 lse.1.given_ref
  49.3 3.5 %collective-permute-done.19.first_ref = bf16[8,272,128]{2,1,0:T(8,128)(2,1)S(1)} collective-permute-done((bf16[8,272,128]{2,1,0:T(8,128)(2,1)S(1)}, bf16[8,272,128]{2,1,0:T(8,128)(2,1)S(1)}, u32[]{:S(2)}, u32[]{:S(2)}) %collective-permute-start.19) | collective-permute-done | bytes 557088 | tf_op jit(solution)/shard_map/ppermute | solution.py:645
  52.7 2.3 %first.1 = (f32[8,128,128]{2,1,0:T(8,128)S(1)}, f32[8,128,128]{2,1,0:T(8,128)S(1)}, f32[8,128,128]{2,1,0:T(8,128)S(1)}, f32[8,128,128]{2,1,0:T(8,128)S(1)}, f32[8,128,128]{2,1,0:T(8,128)S(1)}) custom-call(s32[24]{0:T(128)S(1)} %get-tuple-element.321.table_ref, bf16[8,272,128]{2,1,0:T(8,128)(2,1)S(1)} %get-tuple-element.325.query_side_ref, ...), custom_call_target="tpu_custom_call" | custom-call | flops 671088640 | bytes 4194304 | tf_op jit(solution)/shard_map/first/pallas_call | solution.py:473
  55.0 0.8 collective-permute-done.20.second_ref
  55.9 2.4 %second.1 = (f32[8,128,128]{2,1,0:T(8,128)S(1)}, f32[8,128,128]{2,1,0:T(8,128)S(1)}, f32[8,128,128]{2,1,0:T(8,128)S(1)}, bf16[2,8,128,128]{3,2,1,0:T(8,128)(2,1)S(1)}) custom-call(s32[24]{0:T(128)S(1)} %get-tuple-element.321.table_ref, bf16[8,272,128]{2,1,0:T(8,128)(2,1)S(1)} %get-tuple-element.326.key_side_ref, ...), custom_call_target="tpu_custom_call" | custom-call | flops 671088640 | bytes 4194304 | tf_op jit(solution)/shard_map/second/pallas_call | solution.py:473
  58.3 3.5 %collective-permute-start.22 = (bf16[2,8,128,128]{3,2,1,0:T(8,128)(2,1)S(1)}, bf16[2,8,128,128]{3,2,1,0:T(8,128)(2,1)}, u32[]{:S(2)}, u32[]{:S(2)}) collective-permute-start(bf16[2,8,128,128]{3,2,1,0:T(8,128)(2,1)S(1)} %get-tuple-element.343), channel_id=1, source_target_pairs={{0,48},{64,448},{1,49},{65,449},{2,50},{66,450},{3,51},{67,451},{4... | collective-permute-start | bytes 1572872 | tf_op jit(solution)/shard_map/ppermute | solution.py:645
  61.8 2.3 %third.1 = (f32[8,128,128]{2,1,0:T(8,128)S(1)}, f32[8,128,128]{2,1,0:T(8,128)S(1)}, bf16[8,128,128]{2,1,0:T(8,128)(2,1)S(1)}) custom-call(s32[24]{0:T(128)S(1)} %get-tuple-element.321.table_ref, bf16[8,272,128]{2,1,0:T(8,128)(2,1)S(1)} %get-tuple-element.326.key_side_ref, bf16[8,272,128]{2,1,0:T(8,128)(2,1)S(1)} %collective-permute-done.20.second_ref, ...), custom_call_target="tpu_custom_call" | custom-call | flops 2684354560 | bytes 4194304 | tf_op jit(solution)/shard_map/third/pallas_call | solution.py:473
  64.1 1.9 %collective-permute-start.21 = (bf16[8,128,128]{2,1,0:T(8,128)(2,1)S(1)}, bf16[8,128,128]{2,1,0:T(8,128)(2,1)}, u32[]{:S(2)}, u32[]{:S(2)}) collective-permute-start(bf16[8,128,128]{2,1,0:T(8,128)(2,1)S(1)} %get-tuple-element.342), channel_id=1, source_target_pairs={{0,16},{64,192},{1,17},{65,193},{2,18},{66,194},{3,19},{67,195},{4... | collective-permute-start | bytes 786440 | tf_op jit(solution)/shard_map/ppermute | solution.py:645
  66.0 1.1 %slice.3 = s32[64]{0:T(128)S(1)} slice(s32[65536]{0:T(1024)} %positions_ref.1), slice={[0:65536:1024]} | slice | bytes 512 | tf_op jit(solution)/shard_map/slice | solution.py:712
  67.1 0.6 reduce_max.9
  68.4 3.6 %own.1 = (f32[8,128,128]{2,1,0:T(8,128)S(1)}, f32[8,128,128]{2,1,0:T(8,128)S(1)}, f32[8,128,128]{2,1,0:T(8,128)S(1)}) custom-call(s32[24]{0:T(128)S(1)} %get-tuple-element.321.table_ref, s32[1]{0:T(128)} %bitcast.33._, bf16[8,272,128]{2,1,0:T(8,128)(2,1)S(1)} %get-tuple-element.325.query_side_ref, bf16[8,272,128]{2,1,0:T(8,128)(2,1)S(1)} %get-tuple-element.326.key_side_ref, ...), custom_call_target="tpu_custom_call" | custom-call | flops 1 | bytes 1 | tf_op jit(solution)/shard_map/own/pallas_call | solution.py:473
  72.0 0.5 collective-permute-done.21
  72.5 0.0 collective-permute-done.22
  72.5 25.5 %conditional.1 = ((bf16[128,1024]{1,0:T(8,128)(2,1)}, bf16[128,1024]{1,0:T(8,128)(2,1)}, bf16[128,1024]{1,0:T(8,128)(2,1)})) conditional(s32[]{:T(128)} %convert_element_type.73, (s32[24]{0:T(128)S(1)}, f32[8,128,128]{2,1,0:T(8,128)S(1)}, f32[8,128,128]{2,1,0:T(8,128)S(1)}, f32[8,128,128]{2,1,0:T(8,128)S(1)}, bf16[8,128,128]{2,1,0:T(8,128)(2,1)}, ...), branch_computations={%region_1.0_spmd, %region_2.12_spmd} | conditional | flops 2704931840 | bytes 145718912 | solution.py:792
  72.5 1.4 %join.1 = bf16[4,2,384,128]{3,2,1,0:T(8,128)(2,1)S(1)} custom-call(s32[24]{0:T(128)S(1)} %get-tuple-element.218.table_ref, f32[8,128,128]{2,1,0:T(8,128)S(1)} %get-tuple-element.219.grad_query_ref, f32[8,128,128]{2,1,0:T(8,128)S(1)} %get-tuple-element.220.grad_key_ref, f32[8,128,128]{2,1,0:T(8,128)S(1)} %get-tuple-element.221.grad_value_ref, ...), custom_call_target="tpu_custom_call" | custom-call | bytes 4194304 | tf_op jit(solution)/shard_map/cond/branch_0_fun/join/pallas_call | solution.py:473
  73.9 18.2 %all_to_all.122.slots_ref = bf16[4,2,384,128]{3,2,1,0:T(8,128)(2,1)S(1)} all-to-all(bf16[4,2,384,128]{3,2,1,0:T(8,128)(2,1)S(1)} %join.1), channel_id=1, replica_groups={{0,128,256,384},{1,129,257,385},{2,130,258,386},{3,131,259,387},{4,132,..., dimensions={0} | all-to-all | bytes 1572864 | tf_op jit(solution)/shard_map/cond/branch_0_fun/all_to_all | solution.py:668
  92.1 0.1 turn.1
  92.2 4.7 %all_to_all.123.moved_ref = bf16[2,4,384,128]{3,2,1,0:T(8,128)(2,1)S(1)} all-to-all(bf16[2,4,384,128]{3,2,1,0:T(8,128)(2,1)S(1)} %turn.1), channel_id=1, replica_groups={{0,64},{1,65},{2,66},{3,67},{4,68},{5,69},{6,70},{7,71},{8,72},{9,73},{..., dimensions={0} | all-to-all | bytes 1572864 | tf_op jit(solution)/shard_map/cond/branch_0_fun/all_to_all | solution.py:668
  96.8 1.1 %unpack.1 = (bf16[128,1024]{1,0:T(8,128)(2,1)}, bf16[128,1024]{1,0:T(8,128)(2,1)}, bf16[128,1024]{1,0:T(8,128)(2,1)}) custom-call(bf16[2,4,384,128]{3,2,1,0:T(8,128)(2,1)S(1)} %all_to_all.123.moved_ref), custom_call_target="tpu_custom_call" | custom-call | bytes 4194304 | tf_op jit(solution)/shard_map/cond/branch_0_fun/unpack/pallas_call | solution.py:473
  (2 shorter events, 0.0 us)
Async XLA Ops:
  0.6 7.5 %copy-start.29 = (f32[1024,1]{0,1:T(1,128)S(1)}, f32[1024,1]{0,1:T(1,128)}, u32[]{:S(2)}) copy-start(f32[1024,1]{0,1:T(1,128)} %param.22) | copy-start | bytes 12292
  40.1 12.6 %collective-permute-start.19 = (bf16[8,272,128]{2,1,0:T(8,128)(2,1)S(1)}, bf16[8,272,128]{2,1,0:T(8,128)(2,1)S(1)}, u32[]{:S(2)}, u32[]{:S(2)}) collective-permute-start(bf16[8,272,128]{2,1,0:T(8,128)(2,1)S(1)} %get-tuple-element.327), channel_id=1, source_target_pairs={{0,48},{64,192},{1,49},{65,193},{2,50},{66,194},{3,51},{67,195},{4... | collective-permute-start | bytes 1671176 | tf_op jit(solution)/shard_map/ppermute | solution.py:645
  44.4 11.4 %collective-permute-start.20 = (bf16[8,272,128]{2,1,0:T(8,128)(2,1)S(1)}, bf16[8,272,128]{2,1,0:T(8,128)(2,1)S(1)}, u32[]{:S(2)}, u32[]{:S(2)}) collective-permute-start(bf16[8,272,128]{2,1,0:T(8,128)(2,1)S(1)} %get-tuple-element.329), channel_id=1, source_target_pairs={{0,16},{64,448},{1,17},{65,449},{2,18},{66,450},{3,19},{67,451},{4... | collective-permute-start | bytes 1671176 | tf_op jit(solution)/shard_map/ppermute | solution.py:645
  46.7 2.0 %collective-permute-start.16 = (f32[4,8,128]{2,1,0:T(8,128)S(1)}, f32[4,8,128]{2,1,0:T(8,128)S(1)}, u32[]{:S(2)}, u32[]{:S(2)}) collective-permute-start(f32[4,8,128]{2,1,0:T(8,128)S(1)} %get-tuple-element.323.run_lse_ref), channel_id=1, source_target_pairs={{64,192},{65,193},{66,194},{67,195},{68,196},{69,197},{70,198},{71... | collective-permute-start | bytes 49160 | tf_op jit(solution)/shard_map/ppermute | solution.py:656
  47.3 1.4 %collective-permute-start.17 = (f32[4,8,128]{2,1,0:T(8,128)S(1)}, f32[4,8,128]{2,1,0:T(8,128)S(1)}, u32[]{:S(2)}, u32[]{:S(2)}) collective-permute-start(f32[4,8,128]{2,1,0:T(8,128)S(1)} %get-tuple-element.323.run_lse_ref), channel_id=1, source_target_pairs={{64,320},{65,321},{66,322},{67,323},{68,324},{69,325},{70,326},{71... | collective-permute-start | bytes 49160 | tf_op jit(solution)/shard_map/ppermute | solution.py:656
  48.0 0.7 collective-permute-start.18
  58.3 14.2 %collective-permute-start.22 = (bf16[2,8,128,128]{3,2,1,0:T(8,128)(2,1)S(1)}, bf16[2,8,128,128]{3,2,1,0:T(8,128)(2,1)}, u32[]{:S(2)}, u32[]{:S(2)}) collective-permute-start(bf16[2,8,128,128]{3,2,1,0:T(8,128)(2,1)S(1)} %get-tuple-element.343), channel_id=1, source_target_pairs={{0,48},{64,448},{1,49},{65,449},{2,50},{66,450},{3,51},{67,451},{4... | collective-permute-start | bytes 1572872 | tf_op jit(solution)/shard_map/ppermute | solution.py:645
  64.1 8.4 %collective-permute-start.21 = (bf16[8,128,128]{2,1,0:T(8,128)(2,1)S(1)}, bf16[8,128,128]{2,1,0:T(8,128)(2,1)}, u32[]{:S(2)}, u32[]{:S(2)}) collective-permute-start(bf16[8,128,128]{2,1,0:T(8,128)(2,1)S(1)} %get-tuple-element.342), channel_id=1, source_target_pairs={{0,16},{64,192},{1,17},{65,193},{2,18},{66,194},{3,19},{67,195},{4... | collective-permute-start | bytes 786440 | tf_op jit(solution)/shard_map/ppermute | solution.py:645
